TPU v7x, 512 devices: a whole 4x8x8 slice. The times are simulated.
512 devices in a mesh: rep: 32 (over y, x_lo, core), fsdp: 16 (over x_hi, z).
Axes of the slice: x: 4 (x_hi: 2, x_lo: 2; x = x_hi * 2 + x_lo), y: 8, z: 8, core: 2. Of those that a mesh axis runs over, the one named last changes fastest.
Arguments:
- tokens: bfloat16 [32, 2048, 4096], P('rep', 'fsdp'), may hold values from -6 to 6
- cotangent: bfloat16 [32, 2048, 512], P('rep', 'fsdp'), may hold values from -6 to 6
- params: bfloat16 [32, 4096, 512], P('rep', 'fsdp'), may hold values from -0.09375 to 0.09375
- first_moment: float32 [32, 4096, 512], P('rep', 'fsdp'), may hold values from -0.12 to 0.12
- second_moment: float32 [32, 4096, 512], P('rep', 'fsdp'), may hold values from 0.0001 to 0.001
- weight: bfloat16 [32], P('rep'), may hold values from 0.5 to 2
- step: int32 [1], replicated, may hold values from 0 to 999
Outputs:
- keys: bfloat16 [32, 2048, 512], P('rep', 'fsdp')
- token_grad: bfloat16 [32, 2048, 4096], P('rep', 'fsdp')
- new_params: bfloat16 [32, 4096, 512], P('rep', 'fsdp')
- new_first: float32 [32, 4096, 512], P('rep', 'fsdp')
- new_second: float32 [32, 4096, 512], P('rep', 'fsdp')
- new_weight: float32 [32], P('rep')
All inputs are finite; a program needn't handle non-finite values.
Results may differ from a plain program's by a relative error of at most 0.008.
Values may be sent and summed in bfloat16 or wider, within the bound.
No kernel may reach another device: no remote copies, remote signals or barrier semaphores. Data moves between devices by JAX's collectives and lax.ppermute only.
A program may use at most 64 MiB of HBM per device.

v0:
```python
from functools import partial

import jax
import jax.numpy as jnp
from jax import lax
from jax.sharding import PartitionSpec as P

LEARN = 0.002
BETA_ONE = 0.9
BETA_TWO = 0.999
EPSILON = 1e-08


def for_sending(x):

    def short(part):
        return part.astype(jnp.bfloat16) if part.dtype == jnp.float32 else part

    return jax.tree.map(short, x)


def from_behind(value, axis, steps):
    count = lax.axis_size(axis)
    pairs = [(source, (source + steps) % count) for source in range(count)]
    return lax.ppermute(value, axis, pairs)


def pushed(outgoing, mass_half, hop):
    if hop == 0:
        return (outgoing, mass_half)
    return (
        from_behind(for_sending(outgoing), "rep", hop).astype(outgoing.dtype),
        from_behind(for_sending(mass_half), "rep", hop).astype(mass_half.dtype),
    )


def body(tokens, cotangent, params, first_moment, second_moment, weight, step):
    tok_rows = tokens[0]
    cot_rows = cotangent[0]
    numer = params[0]
    mass = weight.astype(jnp.float32)[0]
    debiased = (numer.astype(jnp.float32) / mass).astype(jnp.bfloat16)
    group_size = lax.axis_size("fsdp")
    total_tokens = tok_rows.shape[0] * group_size
    contract_last = (((1,), (1,)), ((), ()))
    contract_first = (((0,), (0,)), ((), ()))
    columns = tok_rows
    keys = jnp.dot(
        columns,
        lax.all_gather(debiased, "fsdp", axis=0, tiled=True),
        preferred_element_type=jnp.float32,
    )
    token_grad = lax.dot_general(
        cot_rows,
        lax.all_gather(debiased, "fsdp", axis=0, tiled=True),
        contract_last,
        preferred_element_type=jnp.float32,
    )
    columns = tok_rows
    grad_sum = lax.psum_scatter(
        lax.dot_general(
            columns, cot_rows, contract_first, preferred_element_type=jnp.float32
        ).astype(jnp.bfloat16),
        "fsdp",
        scatter_dimension=0,
        tiled=True,
    ).astype(jnp.float32)
    grad = grad_sum / jnp.float32(total_tokens)
    tstep = step[0]
    count = (tstep + 1).astype(jnp.float32)
    bias_one = 1.0 - jnp.power(jnp.float32(BETA_ONE), count)
    bias_two = 1.0 - jnp.power(jnp.float32(BETA_TWO), count)
    new_first = BETA_ONE * first_moment[0] + (1.0 - BETA_ONE) * grad
    new_second = BETA_TWO * second_moment[0] + (1.0 - BETA_TWO) * grad * grad
    update = LEARN * (new_first / bias_one) / (jnp.sqrt(new_second / bias_two) + EPSILON)
    outgoing = (numer.astype(jnp.float32) - update).astype(jnp.bfloat16)
    cycle_size = lax.axis_size("rep")
    branches = [partial(pushed, hop=2**level % cycle_size) for level in range(4)]
    incoming, mass_in = lax.switch(tstep % 4, branches, outgoing, weight)
    new_params = ((outgoing.astype(jnp.float32) + incoming.astype(jnp.float32)) * 0.5).astype(
        jnp.bfloat16
    )
    new_weight = (weight.astype(jnp.float32) + mass_in.astype(jnp.float32)) * 0.5
    return (
        keys.astype(jnp.bfloat16)[None],
        token_grad.astype(jnp.bfloat16)[None],
        new_params[None],
        new_first[None],
        new_second[None],
        new_weight,
    )


def solution(mesh):
    return jax.shard_map(
        body,
        mesh=mesh,
        in_specs=(
            P("rep", "fsdp", None),
            P("rep", "fsdp", None),
            P("rep", "fsdp", None),
            P("rep", "fsdp", None),
            P("rep", "fsdp", None),
            P("rep"),
            P(),
        ),
        out_specs=(
            P("rep", "fsdp", None),
            P("rep", "fsdp", None),
            P("rep", "fsdp", None),
            P("rep", "fsdp", None),
            P("rep", "fsdp", None),
            P("rep"),
        ),
        check_vma=False,
    )
```

profile of v0, /device:TPU:1, one launch (start us, length us, event | category | flops | bytes accessed | tf_op | source)
XLA Modules:
  0.0 354.5 jit_solution(15512093780668596089)
XLA Ops:
  7.2 0.0 copy-start
  7.2 0.0 reduce-scatter.2.cloned.1.call-start
  7.2 1.2 copy-done
  8.4 4.1 %convolution_convert_fusion = bf16[4096,512]{1,0:T(8,128)(2,1)} fusion(bf16[1,128,4096]{2,1,0:T(8,128)(2,1)S(1)} %copy-done, bf16[1,128,512]{2,1,0:T(8,128)(2,1)} %param.12), kind=kOutput, calls=%fused_computation | convolution fusion | flops 538968064 | bytes 5373952 | tf_op jit(solution)/shard_map/dot_general | solution.py:61
  12.5 0.0 copy-start.2
  12.5 0.0 copy-start.3
  12.5 0.0 copy-start.4
  12.5 0.0 copy-start.1
  12.5 0.0 reduce-scatter.2.cloned.1.call-update
  12.6 0.0 all-gather.2.cloned.1.call-start
  14.1 214.2 %reduce-scatter.2.cloned.1.call-done = bf16[256,512]{1,0:T(8,128)(2,1)} async-done(((bf16[4096,512]{1,0:T(8,128)(2,1)}), bf16[256,512]{1,0:T(8,128)(2,1)}) %reduce-scatter.2.cloned.1.call-update) | async-done | bytes 262160 | tf_op jit(solution)/shard_map/reduce_scatter | solution.py:60
  228.3 0.0 copy-done.2
  228.3 0.0 copy-done.3
  228.3 0.0 copy-done.4
  228.3 2.3 fusion.13
  230.6 0.0 all-gather.2.cloned.1.call-update
  230.7 9.4 %conditional.4 = (bf16[256,512]{1,0:T(8,128)(2,1)}, bf16[1]{0:T(256)(128)(2,1)}) conditional(s32[]{:T(128)} %clamp.3, (bf16[256,512]{1,0:T(8,128)(2,1)S(1)}, bf16[1]{0:T(256)(128)(2,1)}) %tuple.50, (bf16[256,512]{1,0:T(8,128)(2,1)S(1)}, bf16[1]{0:T(256)(128)(2,1)}) %tuple.50, (bf16[256,512]{1,0:T(8,128)(2,1)S(1)}, ...), branch_computations={%region_1.2_spmd, %region_2.3_spmd, %region_3.4_spmd, %region_4.5_... | conditional | bytes 1048680
  230.7 2.4 collective-permute-start.2
  233.1 3.9 %collective-permute-start.3 = (bf16[1]{0:T(256)(128)(2,1)}, bf16[1]{0:T(256)(128)(2,1)}, u32[]{:S(2)}, u32[]{:S(2)}) collective-permute-start(bf16[1]{0:T(256)(128)(2,1)} %get-tuple-element.31), channel_id=1, source_target_pairs={{0,32},{16,48},{32,64},{48,80},{64,96},{80,112},{96,128},{112,144}... | collective-permute-start | bytes 14 | tf_op jit(solution)/shard_map/cond/branch_1_fun/ppermute | solution.py:25
  237.0 3.1 collective-permute-done.3
  240.1 0.0 collective-permute-done.2
  240.7 1.7 fusion.12
  242.5 95.1 %all-gather.2.cloned.1.call-done = bf16[4096,512]{1,0:T(8,128)(2,1)} async-done(((bf16[256,512]{1,0:T(8,128)(2,1)}), bf16[4096,512]{1,0:T(8,128)(2,1)}) %all-gather.2.cloned.1.call-update) | async-done | bytes 4194320 | tf_op jit(solution)/shard_map/all_gather | solution.py:50
  337.5 0.0 copy-done.1
  337.5 3.4 fusion
  341.0 1.3 copy.14
  342.3 3.5 fusion.1
  345.8 0.8 copy.13
Async XLA Ops:
  7.2 1.2 copy-start
  7.2 221.1 %reduce-scatter.2.cloned.1.call-start = ((), (), s32[]{:S(2)}) async-start(), calls=%async_computation.2 | async-start | bytes 4456448 | tf_op jit(solution)/shard_map/reduce_scatter | solution.py:60
  12.5 215.8 %copy-start.2 = (f32[1,256,512]{2,1,0:T(8,128)S(1)}, f32[1,256,512]{2,1,0:T(8,128)}, u32[]{:S(2)}) copy-start(f32[1,256,512]{2,1,0:T(8,128)} %param.15) | copy-start | bytes 1572868
  12.5 215.8 %copy-start.3 = (f32[1,256,512]{2,1,0:T(8,128)S(1)}, f32[1,256,512]{2,1,0:T(8,128)}, u32[]{:S(2)}) copy-start(f32[1,256,512]{2,1,0:T(8,128)} %param.14) | copy-start | bytes 1572868
  12.5 215.8 %copy-start.4 = (bf16[1,256,512]{2,1,0:T(8,128)(2,1)S(1)}, bf16[1,256,512]{2,1,0:T(8,128)(2,1)}, u32[]{:S(2)}) copy-start(bf16[1,256,512]{2,1,0:T(8,128)(2,1)} %param.13) | copy-start | bytes 786436
  12.5 325.0 %copy-start.1 = (bf16[1,128,512]{2,1,0:T(8,128)(2,1)S(1)}, bf16[1,128,512]{2,1,0:T(8,128)(2,1)}, u32[]{:S(2)}) copy-start(bf16[1,128,512]{2,1,0:T(8,128)(2,1)} %param.12) | copy-start | bytes 393220
  12.6 325.0 %all-gather.2.cloned.1.call-start = ((), (), s32[]{:S(2)}) async-start(), calls=%async_computation.1 | async-start | bytes 4456448 | tf_op jit(solution)/shard_map/all_gather | solution.py:50
  230.7 9.4 %collective-permute-start.2 = (bf16[256,512]{1,0:T(8,128)(2,1)S(1)}, bf16[256,512]{1,0:T(8,128)(2,1)}, u32[]{:S(2)}, u32[]{:S(2)}) collective-permute-start(bf16[256,512]{1,0:T(8,128)(2,1)S(1)} %get-tuple-element.30), channel_id=1, source_target_pairs={{0,32},{16,48},{32,64},{48,80},{64,96},{80,112},{96,128},{112,144}... | collective-permute-start | bytes 786440 | tf_op jit(solution)/shard_map/cond/branch_1_fun/ppermute | solution.py:25
  233.1 7.0 %collective-permute-start.3 = (bf16[1]{0:T(256)(128)(2,1)}, bf16[1]{0:T(256)(128)(2,1)}, u32[]{:S(2)}, u32[]{:S(2)}) collective-permute-start(bf16[1]{0:T(256)(128)(2,1)} %get-tuple-element.31), channel_id=1, source_target_pairs={{0,32},{16,48},{32,64},{48,80},{64,96},{80,112},{96,128},{112,144}... | collective-permute-start | bytes 14 | tf_op jit(solution)/shard_map/cond/branch_1_fun/ppermute | solution.py:25
Sparse Core Ops, SparseCore 0:
  12.7 215.5 reduce-scatter.1
  232.5 104.9 all-gather.1
where the time goes:
time: 357 us; the launch traced here: 355 us
  waiting for transfers between devices  312 us (87%)
  between operations  17.3 us (5%)
  matrix products  11 us (3%)
  starting transfers between devices  6.4 us (2%)
  other arithmetic  4.05 us (1%)
    reduce_scatter x1, waiting for transfers between devices, body(): lax.psum_scatter(lax.dot_general(columns, cot_rows, contract_first, prefe...  214 us
    all_gather x1, waiting for transfers between devices, body(): lax.all_gather(debiased, 'fsdp', axis=0, tiled=True)  95.1 us
  transfers between devices with their start and end apart: 4, of which 3 were waited for; matrix products, arithmetic and copies ran while one was open for 0% of the time, Pallas kernels for 0%

commit v1 on v0

v1 whole, which is shorter than its diff:
```python
from functools import partial

import jax
import jax.numpy as jnp
from jax import lax
from jax.sharding import Mesh, PartitionSpec as P

LEARN = 0.002
BETA_ONE = 0.9
BETA_TWO = 0.999
EPSILON = 1e-08
GROUP = ("xh", "zq", "zp")
REPS = ("y", "xl", "c")
PAIRS = ("c", "xh", "zq", "zp")


def feature_groups():
    groups = []
    for core in range(2):
        for k in range(4):
            even = 2 * k if core == 0 else (2 * k + 2) % 8
            odd = 2 * k + 1
            groups.append([core * 16 + xh * 8 + z for xh in range(2) for z in (even, odd)])
    return groups


def swap_features(x):
    return lax.all_to_all(x, PAIRS, 0, 0, axis_index_groups=feature_groups(), tiled=True)


def swap_tokens(x):
    return lax.all_to_all(x, "zq", 0, 0, tiled=True)


def pushed(outgoing, hop):
    pairs = [(source, (source + hop) % 32) for source in range(32)]
    return lax.ppermute(outgoing, REPS, pairs)


def body(tokens, cotangent, params, first_moment, second_moment, weight, step):
    numer = params[0].astype(jnp.float32)
    mass = weight.astype(jnp.float32)[0]
    debiased = (numer / mass).astype(jnp.bfloat16)
    rows = swap_tokens(jnp.broadcast_to(debiased, (4, 256, 512))).reshape(1024, 512)

    columns = tokens[0].reshape(128, 2, 4, 2, 256).transpose(1, 3, 0, 2, 4).reshape(4, 128, 1024)
    out = jnp.concatenate([columns, jnp.broadcast_to(cotangent[0], (4, 128, 512))], axis=2)
    got = swap_features(out).reshape(512, 1536)
    tok, cot = got[:, :1024], got[:, 1024:]

    share = lax.dot_general(tok, cot, (((0,), (0,)), ((), ())), preferred_element_type=jnp.float32)
    shares = swap_tokens(share.astype(jnp.bfloat16).reshape(4, 256, 512))

    keys = jnp.dot(tok, rows, preferred_element_type=jnp.float32).astype(jnp.bfloat16)
    token_grad = lax.dot_general(
        cot, rows, (((1,), (1,)), ((), ())), preferred_element_type=jnp.float32
    ).astype(jnp.bfloat16)
    back = swap_features(
        jnp.concatenate([token_grad, keys], axis=1).reshape(4, 128, 1536)
    )
    keys = back[:, :, 1024:].astype(jnp.float32).sum(axis=0).astype(jnp.bfloat16)
    token_grad = (
        back[:, :, :1024].reshape(2, 2, 128, 4, 256).transpose(2, 0, 3, 1, 4).reshape(128, 4096)
    )

    grad = shares.astype(jnp.float32).sum(axis=0) / jnp.float32(2048)
    tstep = step[0]
    count = (tstep + 1).astype(jnp.float32)
    bias_one = 1.0 - jnp.power(jnp.float32(BETA_ONE), count)
    bias_two = 1.0 - jnp.power(jnp.float32(BETA_TWO), count)
    new_first = BETA_ONE * first_moment[0] + (1.0 - BETA_ONE) * grad
    new_second = BETA_TWO * second_moment[0] + (1.0 - BETA_TWO) * grad * grad
    update = LEARN * (new_first / bias_one) / (jnp.sqrt(new_second / bias_two) + EPSILON)
    outgoing = (numer - update).astype(jnp.bfloat16)
    sent = jnp.concatenate([outgoing, jnp.broadcast_to(weight[0], (16, 512))], axis=0)
    branches = [partial(pushed, hop=2**level) for level in range(4)]
    incoming = lax.switch(tstep % 4, branches, sent)
    new_params = (
        (outgoing.astype(jnp.float32) + incoming[:256].astype(jnp.float32)) * 0.5
    ).astype(jnp.bfloat16)
    new_weight = (weight.astype(jnp.float32) + incoming[256, :1].astype(jnp.float32)) * 0.5
    return (
        keys[None],
        token_grad[None],
        new_params[None],
        new_first[None],
        new_second[None],
        new_weight,
    )


def solution(mesh):
    fine = Mesh(mesh.devices.reshape(8, 2, 2, 2, 4, 2), REPS + GROUP)
    rows = P(REPS, GROUP, None)
    return jax.shard_map(
        body,
        mesh=fine,
        in_specs=(rows, rows, rows, rows, rows, P(REPS), P()),
        out_specs=(rows, rows, rows, rows, rows, P(REPS)),
        check_vma=False,
    )
```

time: 357 us -> 141 us (0.39)
  waiting for transfers between devices: 312 us -> 30.3 us
  blocking collectives: 0 us -> 50.6 us
  starting transfers between devices: 6.4 us -> 29.4 us
  between operations: 17.3 us -> 3.95 us
  local copies, waits for them, and re-layouts: 3.28 us -> 14.4 us
  matrix products: 11 us -> 4.52 us
    reduce_scatter x1 -> x0, waiting for transfers between devices: 214 us -> none  [body(): lax.psum_scatter(lax.dot_general(columns, cot_rows, contract_first, prefe...]
    all_gather x1 -> x0, waiting for transfers between devices: 95.1 us -> none  [body(): lax.all_gather(debiased, 'fsdp', axis=0, tiled=True)]
    all_to_all x0 -> x2, blocking collectives: none -> 50.6 us  [the longest x1 30.8 us: swap_features(): lax.all_to_all(x, PAIRS, 0, 0, axis_index_groups=feature_groups(), tiled=...]
    all_to_all x0 -> x2, starting transfers between devices: none -> 23.9 us  [the longest x1 20.3 us: swap_features(): lax.all_to_all(x, PAIRS, 0, 0, axis_index_groups=feature_groups(), tiled=...]
    all_to_all x0 -> x2, waiting for transfers between devices: none -> 15.8 us  [the longest x1 15.8 us: swap_tokens(): return lax.all_to_all(x, 'zq', 0, 0, tiled=True)]
    ppermute x2 -> x1, waiting for transfers between devices: 3.06 us -> 14.5 us  [pushed(): return lax.ppermute(outgoing, REPS, pairs)]
    dot_general x3, matrix products: 11 us -> 4.52 us  [the longest x1 3.08 us: body(): lax.dot_general(tok, cot, (((0,), (0,)), ((), ())), preferred_element_typ...]
    reshape x0 -> x2, local copies, waits for them, and re-layouts: none -> 4.44 us  [body(): back[:, :, :1024].reshape(2, 2, 128, 4, 256).transpose(2, 0, 3, 1, 4)]
  transfers between devices with their start and end apart: 4 -> 3, of which waited for: 3 -> 2; matrix products, arithmetic and copies ran while one was open for 0% -> 3% of each run, Pallas kernels for 0% -> 0%
where the time goes in v1:
time: 141 us; the launch traced here: 139 us
  blocking collectives  50.6 us (36%)
  waiting for transfers between devices  30.3 us (21%)
  starting transfers between devices  29.4 us (21%)
  local copies, waits for them, and re-layouts  14.4 us (10%)
  other arithmetic  5.58 us (4%)
  matrix products  4.52 us (3%)
  between operations  3.95 us (3%)
    all_to_all x1, blocking collectives, swap_features(): lax.all_to_all(x, PAIRS, 0, 0, axis_index_groups=feature_groups(), tiled=...  30.8 us
    all_to_all x1, starting transfers between devices, swap_features(): lax.all_to_all(x, PAIRS, 0, 0, axis_index_groups=feature_groups(), tiled=...  20.3 us
    all_to_all x1, blocking collectives, swap_tokens(): return lax.all_to_all(x, 'zq', 0, 0, tiled=True)  19.8 us
    all_to_all x1, waiting for transfers between devices, swap_tokens(): return lax.all_to_all(x, 'zq', 0, 0, tiled=True)  15.8 us
    ppermute x1, waiting for transfers between devices, pushed(): return lax.ppermute(outgoing, REPS, pairs)  14.5 us
    ppermute x1, starting transfers between devices, pushed(): return lax.ppermute(outgoing, REPS, pairs)  5.42 us
    reshape x2, local copies, waits for them, and re-layouts, body(): back[:, :, :1024].reshape(2, 2, 128, 4, 256).transpose(2, 0, 3, 1, 4)  4.44 us
    all_to_all x1, starting transfers between devices, swap_tokens(): return lax.all_to_all(x, 'zq', 0, 0, tiled=True)  3.65 us
  transfers between devices with their start and end apart: 3, of which 2 were waited for; matrix products, arithmetic and copies ran while one was open for 3% of the time, Pallas kernels for 0%

profile of v1, /device:TPU:1, one launch (start us, length us, event | category | flops | bytes accessed | tf_op | source)
XLA Modules:
  0.0 138.7 jit_solution(14488997475522619583)
XLA Ops:
  0.6 1.6 %copy.18 = bf16[1,128,4096]{1,2,0:T(8,128)(2,1)S(1)} copy(bf16[1,128,4096]{2,1,0:T(8,128)(2,1)} %param.11) | data formatting | bytes 2097152 | tf_op args[0]
  2.3 0.0 copy-start.4
  2.3 0.1 copy.19
  2.4 0.8 copy-done.4
  3.2 0.1 copy.20
  3.3 0.1 broadcast_in_dim.15
  3.4 0.1 pad_maximum_fusion
  3.5 30.8 %all_to_all.20 = bf16[4,128,1536]{1,2,0:T(8,128)(2,1)S(1)} all-to-all(bf16[4,128,1536]{1,2,0:T(8,128)(2,1)S(1)} %pad_maximum_fusion), channel_id=1, replica_groups={{0,1,8,9},{2,3,10,11},{4,5,12,13},{6,7,14,15},{18,17,26,25},{20,19,28,2..., dimensions={0} | all-to-all | bytes 3145728 | tf_op jit(solution)/shard_map/all_to_all | solution.py:28
  34.2 1.6 %copy.21 = bf16[4,128,1536]{2,1,0:T(8,128)(2,1)} copy(bf16[4,128,1536]{1,2,0:T(8,128)(2,1)S(1)} %all_to_all.20) | data formatting | bytes 3145728 | tf_op jit(solution)/shard_map/all_to_all | solution.py:28
  35.8 3.1 %convolution_convert_fusion = bf16[1024,512]{1,0:T(8,128)(2,1)} fusion(bf16[512,1536]{1,0:T(8,128)(2,1)} %bitcast.62), kind=kOutput, calls=%fused_computation.3 | convolution fusion | flops 537395200 | bytes 2621440 | tf_op jit(solution)/shard_map/dot_general | solution.py:51
  38.9 3.6 %all-to-all-start.3 = ((bf16[4,256,512]{2,1,0:T(8,128)(2,1)}), bf16[4,256,512]{2,1,0:T(8,128)(2,1)S(1)}, u32[]{:S(2)}, u32[]{:S(2)}) async-start(bf16[4,256,512]{2,1,0:T(8,128)(2,1)} %bitcast.65), calls=%async_computation.3 | async-start | bytes 2097152 | tf_op jit(solution)/shard_map/all_to_all | solution.py:32
  44.0 15.8 %all-to-all-done.3 = bf16[4,256,512]{2,1,0:T(8,128)(2,1)S(1)} async-done(((bf16[4,256,512]{2,1,0:T(8,128)(2,1)}), bf16[4,256,512]{2,1,0:T(8,128)(2,1)S(1)}, u32[]{:S(2)}, u32[]{:S(2)}) %all-to-all-start.3) | async-done | bytes 1048608 | tf_op jit(solution)/shard_map/all_to_all | solution.py:32
  59.8 0.1 convert_reduce_fusion
  60.0 0.5 fusion.3
  60.5 0.1 broadcast_in_dim.16
  60.5 19.8 %all_to_all.21 = bf16[4,256,512]{2,1,0:T(8,128)(2,1)S(1)} all-to-all(bf16[4,256,512]{2,1,0:T(8,128)(2,1)S(1)} %broadcast_in_dim.16), channel_id=1, replica_groups=mesh['y'=8,'xl'=2,'c'=2,'xh'=2,'zq'=4,'zp'=2] {'zq'}, dimensions={0} | all-to-all | bytes 2097152 | tf_op jit(solution)/shard_map/all_to_all | solution.py:32
  80.4 0.7 convolution_convert_fusion.1
  81.1 0.7 convolution_convert_fusion.2
  81.8 1.3 pad_maximum_fusion.1
  83.1 20.3 %all-to-all-start.2 = ((bf16[4,128,1536]{2,1,0:T(8,128)(2,1)}), bf16[4,128,1536]{2,1,0:T(8,128)(2,1)S(1)}, u32[]{:S(2)}, u32[]{:S(2)}) async-start(bf16[4,128,1536]{2,1,0:T(8,128)(2,1)} %bitcast.12), calls=%async_computation.2 | async-start | bytes 3145728 | tf_op jit(solution)/shard_map/all_to_all | solution.py:28
  103.4 20.6 %conditional.1 = (bf16[272,512]{1,0:T(8,128)(2,1)}) conditional(s32[]{:T(128)} %clamp.3, (bf16[256,512]{1,0:T(8,128)(2,1)S(1)}, bf16[1]{0:T(256)(128)(2,1)}) %tuple.21, (bf16[256,512]{1,0:T(8,128)(2,1)S(1)}, bf16[1]{0:T(256)(128)(2,1)}) %tuple.21, (bf16[256,512]{1,0:T(8,128)(2,1)S(1)}, ...), branch_computations={%region_2.3_spmd, %region_3.4_spmd, %region_4.5_spmd, %region_5.6_... | conditional | bytes 1654834 | solution.py:77
  103.4 0.7 concatenate.24
  104.0 5.4 %collective-permute-start = (bf16[272,512]{1,0:T(8,128)(2,1)S(1)}, bf16[272,512]{1,0:T(8,128)(2,1)}, u32[]{:S(2)}, u32[]{:S(2)}) collective-permute-start(bf16[272,512]{1,0:T(8,128)(2,1)S(1)} %concatenate.24), channel_id=1, source_target_pairs={{0,16},{16,32},{32,48},{48,64},{64,80},{80,96},{96,112},{112,128},... | collective-permute-start | bytes 835592 | tf_op jit(solution)/shard_map/cond/branch_0_fun/ppermute | solution.py:37
  109.5 14.5 %collective-permute-done = bf16[272,512]{1,0:T(8,128)(2,1)} collective-permute-done((bf16[272,512]{1,0:T(8,128)(2,1)S(1)}, bf16[272,512]{1,0:T(8,128)(2,1)}, u32[]{:S(2)}, u32[]{:S(2)}) %collective-permute-start) | collective-permute-done | bytes 278560 | tf_op jit(solution)/shard_map/cond/branch_0_fun/ppermute | solution.py:37
  123.9 1.2 slice.29
  125.7 1.7 %fusion.12 = bf16[1,256,512]{2,1,0:T(8,128)(2,1)} fusion(bf16[256,512]{1,0:T(8,128)(2,1)S(1)} %get-tuple-element.29, bf16[272,512]{1,0:T(8,128)(2,1)} %get-tuple-element.31), kind=kLoop, calls=%fused_computation.28 | loop fusion | flops 655360 | bytes 786432 | tf_op jit(solution)/shard_map/broadcast_in_dim | solution.py:85
  127.5 1.2 bitcast_add_fusion
  128.6 1.1 slice.27
  129.8 1.9 %reshape.69 = bf16[2,2,128,4,256]{4,3,2,1,0:T(4,128)(2,1)S(1)} reshape(bf16[4,128,1024]{2,1,0:T(8,128)(2,1)} %slice.27) | data formatting | bytes 2097152 | tf_op jit(solution)/shard_map/reshape | solution.py:63
  131.6 2.6 %copy.26 = bf16[2,2,128,4,256]{4,1,3,0,2:T(2,128)(2,1)} copy(bf16[2,2,128,4,256]{4,3,2,1,0:T(4,128)(2,1)S(1)} %reshape.69) | data formatting | bytes 2097152 | tf_op jit(solution)/shard_map/reshape | solution.py:63
  134.2 2.6 %broadcast_in_dim_reshape.3 = bf16[1,128,4096]{2,1,0:T(8,128)(2,1)} reshape(bf16[128,2,4,2,256]{4,3,2,1,0:T(2,128)(2,1)} %bitcast.60) | data formatting | bytes 2097152 | tf_op jit(solution)/shard_map/broadcast_in_dim;reshape | solution.py:84
  136.8 0.7 slice_reduce_fusion
  (9 shorter events, 0.0 us)
Async XLA Ops:
  2.3 0.9 copy-start.4
  38.9 21.1 %copy-start = (f32[1,256,512]{2,1,0:T(8,128)S(1)}, f32[1,256,512]{2,1,0:T(8,128)}, u32[]{:S(2)}) copy-start(f32[1,256,512]{2,1,0:T(8,128)} %param.15) | copy-start | bytes 1572868
  38.9 21.1 %copy-start.1 = (f32[1,256,512]{2,1,0:T(8,128)S(1)}, f32[1,256,512]{2,1,0:T(8,128)}, u32[]{:S(2)}) copy-start(f32[1,256,512]{2,1,0:T(8,128)} %param.14) | copy-start | bytes 1572868
  38.9 21.1 %copy-start.3 = (bf16[1,256,512]{2,1,0:T(8,128)(2,1)S(1)}, bf16[1,256,512]{2,1,0:T(8,128)(2,1)}, u32[]{:S(2)}) copy-start(bf16[1,256,512]{2,1,0:T(8,128)(2,1)} %param.13) | copy-start | bytes 786436
  38.9 20.9 %all-to-all-start.3 = ((bf16[4,256,512]{2,1,0:T(8,128)(2,1)}), bf16[4,256,512]{2,1,0:T(8,128)(2,1)S(1)}, u32[]{:S(2)}, u32[]{:S(2)}) async-start(bf16[4,256,512]{2,1,0:T(8,128)(2,1)} %bitcast.65), calls=%async_computation.3 | async-start | bytes 2097152 | tf_op jit(solution)/shard_map/all_to_all | solution.py:32
  60.4 19.9 %copy-start.2 = (bf16[4,128,1536]{2,1,0:T(8,128)(2,1)S(1)}, bf16[4,128,1536]{2,1,0:T(8,128)(2,1)}, u32[]{:S(2)}) copy-start(bf16[4,128,1536]{2,1,0:T(8,128)(2,1)} %copy.21) | copy-start | bytes 4718596
  83.1 45.6 %all-to-all-start.2 = ((bf16[4,128,1536]{2,1,0:T(8,128)(2,1)}), bf16[4,128,1536]{2,1,0:T(8,128)(2,1)S(1)}, u32[]{:S(2)}, u32[]{:S(2)}) async-start(bf16[4,128,1536]{2,1,0:T(8,128)(2,1)} %bitcast.12), calls=%async_computation.2 | async-start | bytes 3145728 | tf_op jit(solution)/shard_map/all_to_all | solution.py:28
  104.0 19.9 %collective-permute-start = (bf16[272,512]{1,0:T(8,128)(2,1)S(1)}, bf16[272,512]{1,0:T(8,128)(2,1)}, u32[]{:S(2)}, u32[]{:S(2)}) collective-permute-start(bf16[272,512]{1,0:T(8,128)(2,1)S(1)} %concatenate.24), channel_id=1, source_target_pairs={{0,16},{16,32},{32,48},{48,64},{64,80},{80,96},{96,112},{112,128},... | collective-permute-start | bytes 835592 | tf_op jit(solution)/shard_map/cond/branch_0_fun/ppermute | solution.py:37

commit v2 on v1

v2 whole, which is shorter than its diff:
```python
from functools import partial

import jax
import jax.numpy as jnp
from jax import lax
from jax.experimental import pallas as pl
from jax.experimental.pallas import tpu as pltpu
from jax.sharding import Mesh, PartitionSpec as P

LEARN = 0.002
BETA_ONE = 0.9
BETA_TWO = 0.999
EPSILON = 1e-08
GROUP = ("xh", "zq", "zp")
REPS = ("y", "xl", "c")
PAIRS = ("c", "xh", "zq", "zp")
F32 = jnp.float32
BF16 = jnp.bfloat16


def neighbour(core, z):
    return z ^ 1 if core == 0 else ((z + 1) ^ 1) - 1 & 7


def feature_groups():
    groups = []
    for core in range(2):
        for even in range(0, 8, 2):
            zs = (even, neighbour(core, even))
            groups.append([core * 16 + xh * 8 + z for xh in range(2) for z in zs])
    return groups


def partner_pairs(relative):
    pairs = []
    for core in range(2):
        for xh in range(2):
            for z in range(8):
                to_z = neighbour(core, z) if relative & 1 else z
                to_x = xh ^ (relative >> 1)
                pairs.append((core * 16 + xh * 8 + z, core * 16 + to_x * 8 + to_z))
    return pairs


def along_quad(x, step):
    return lax.ppermute(x, "zq", [(i, (i + step) % 4) for i in range(4)])


def pushed(outgoing, hop):
    pairs = [(source, (source + hop) % 32) for source in range(32)]
    return lax.ppermute(outgoing, REPS, pairs)


VMEM = pl.BlockSpec(memory_space=pltpu.VMEM)
ANY = pl.BlockSpec(memory_space=pl.ANY)
SMEM = pl.BlockSpec(memory_space=pltpu.SMEM)


def params_of(flops=0, moved=0, mib=48):
    return dict(
        compiler_params=pltpu.CompilerParams(vmem_limit_bytes=mib << 20),
        cost_estimate=pl.CostEstimate(flops=flops, bytes_accessed=moved, transcendentals=0),
    )


def pack_kernel(t0, t1, t2, t3, cot, out):
    for q, part in enumerate((t0, t1, t2, t3)):
        out[0, :, q * 256 : (q + 1) * 256] = part[...]
    out[0, :, 1024:] = cot[...]


def pack(tokens, cot):
    columns = [
        pl.BlockSpec((128, 256), lambda c, q=q: (0, (c // 2) * 8 + q * 2 + c % 2)) for q in range(4)
    ]
    return pl.pallas_call(
        pack_kernel,
        grid=(4,),
        in_specs=[*columns, pl.BlockSpec((128, 512), lambda c: (0, 0))],
        out_specs=pl.BlockSpec((1, 128, 1536), lambda c: (c, 0, 0)),
        out_shape=pltpu.HBM((4, 128, 1536), BF16),
        name="pack",
        **params_of(0, 3 << 20),
    )(tokens, tokens, tokens, tokens, cot)


def share_kernel(tok, cot, out):
    out[0] = lax.dot_general(
        tok[...], cot[...], (((0,), (0,)), ((), ())), preferred_element_type=F32
    ).astype(BF16)


def share(got):
    return pl.pallas_call(
        share_kernel,
        grid=(4,),
        in_specs=[pl.BlockSpec((512, 256), lambda q: (0, q)), pl.BlockSpec((512, 512), lambda q: (0, 2))],
        out_specs=pl.BlockSpec((1, 256, 512), lambda q: (q, 0, 0)),
        out_shape=pltpu.HBM((4, 256, 512), BF16),
        name="share",
        **params_of(2 * 512 * 1024 * 512, 5 << 19),
    )(got, got)


def product_kernel(got, own_w, w_down, w_up, far_a, far_b, own, to_z, to_x, to_xz, total):
    place = lax.axis_index("xh") * 2 + lax.axis_index("zp")
    quad = lax.axis_index("zq")
    cot = got[:, 1024:]
    keys = None
    for k, w in enumerate((own_w, w_up, None, w_down)):
        w = jnp.concatenate([far_a[...], far_b[...]], axis=0) if w is None else w[...]
        columns = pl.ds(pl.multiple_of(lax.rem(quad + k, 4) * 256, 256), 256)
        term = jnp.dot(got[:, columns], w, preferred_element_type=F32)
        keys = term if keys is None else keys + term
        total[:, columns] = lax.dot_general(
            cot, w, (((1,), (1,)), ((), ())), preferred_element_type=F32
        ).astype(BF16)
    total[:, 1024:] = keys.astype(BF16)
    for relative, out in enumerate((own, to_z, to_x, to_xz)):
        rows = pl.ds(pl.multiple_of((place ^ relative) * 128, 128), 128)
        out[...] = total[rows, :]


def products(got, own_w, w_down, w_up, far_a, far_b):
    block = jax.ShapeDtypeStruct((128, 1536), BF16)
    return pl.pallas_call(
        product_kernel,
        in_specs=[VMEM] * 6,
        out_specs=[VMEM] * 4,
        out_shape=[block] * 4,
        scratch_shapes=[pltpu.VMEM((512, 1536), BF16)],
        name="products",
        **params_of(4 * 512 * 1024 * 512, 4 << 20),
    )(got, own_w, w_down, w_up, far_a, far_b)


def adam_kernel(weight, bias, shares, first, second, numer, new_first, new_second, sent):
    total = shares[0].astype(F32)
    for q in range(1, 4):
        total = total + shares[q].astype(F32)
    grad = total / 2048.0
    one = BETA_ONE * first[...] + (1.0 - BETA_ONE) * grad
    two = BETA_TWO * second[...] + (1.0 - BETA_TWO) * grad * grad
    new_first[...] = one
    new_second[...] = two
    update = LEARN * (one / bias[0]) / (jnp.sqrt(two / bias[1]) + EPSILON)
    sent[:256, :] = (numer[...].astype(F32) - update).astype(BF16)
    sent[256:, :] = jnp.full((16, 512), weight[0], F32).astype(BF16)


def adam(weight, bias, shares, first, second, numer):
    state = jax.ShapeDtypeStruct((256, 512), F32)
    return pl.pallas_call(
        adam_kernel,
        in_specs=[SMEM, SMEM] + [VMEM] * 4,
        out_specs=[VMEM] * 3,
        out_shape=[state, state, jax.ShapeDtypeStruct((272, 512), BF16)],
        name="adam",
        **params_of(0, 4 << 20),
    )(weight, bias, shares, first, second, numer)


def finish_kernel(sent, incoming, own, from_z, from_x, from_xz, new_params, mixed, token_grad, keys):
    new_params[...] = (
        (sent[:256, :].astype(F32) + incoming[:256, :].astype(F32)) * 0.5
    ).astype(BF16)
    mixed[0] = (jnp.max(sent[256:264, :128].astype(F32)) + jnp.max(incoming[256:264, :128].astype(F32))) * 0.5
    place = lax.axis_index("xh") * 2 + lax.axis_index("zp")
    total = None
    for relative, part in enumerate((own, from_z, from_x, from_xz)):
        cls = place ^ relative
        for q in range(4):
            column = (cls // 2) * 2048 + q * 512 + (cls % 2) * 256
            token_grad[:, pl.ds(pl.multiple_of(column, 256), 256)] = part[:, q * 256 : (q + 1) * 256]
        term = part[:, 1024:].astype(F32)
        total = term if total is None else total + term
    keys[...] = total.astype(BF16)


def finish(sent, incoming, own, from_z, from_x, from_xz):
    return pl.pallas_call(
        finish_kernel,
        in_specs=[VMEM] * 6,
        out_specs=[VMEM, SMEM, VMEM, VMEM],
        out_shape=[
            jax.ShapeDtypeStruct((256, 512), BF16),
            jax.ShapeDtypeStruct((1,), F32),
            jax.ShapeDtypeStruct((128, 4096), BF16),
            jax.ShapeDtypeStruct((128, 512), BF16),
        ],
        name="finish",
        **params_of(0, 4 << 20),
    )(sent, incoming, own, from_z, from_x, from_xz)


def step_with(tokens, cotangent, params, first_moment, second_moment, weight, step, hop):
    mass = weight.astype(F32)
    tstep = step[0]
    count = (tstep + 1).astype(F32)
    bias = 1.0 - jnp.power(jnp.array([BETA_ONE, BETA_TWO], F32), count)

    debiased = (params[0].astype(F32) / mass[0]).astype(BF16)
    out = pack(tokens[0], cotangent[0])
    w_down = along_quad(debiased, 1)
    w_up = along_quad(debiased, -1)
    got = lax.all_to_all(out, PAIRS, 0, 0, axis_index_groups=feature_groups(), tiled=True)
    far_a = along_quad(w_down[:128], 1)
    far_b = along_quad(w_up[128:], -1)
    got, far_a, far_b = lax.optimization_barrier((got.reshape(512, 1536), far_a, far_b))

    shares = lax.all_to_all(share(got), "zq", 0, 0, tiled=True)

    own, *sends = products(got, debiased, w_down, w_up, far_a, far_b)
    back = [lax.ppermute(x, PAIRS, partner_pairs(r + 1)) for r, x in enumerate(sends)]

    new_first, new_second, sent = adam(
        mass, bias, shares, first_moment[0], second_moment[0], params[0]
    )
    incoming = pushed(sent, hop)
    new_params, mixed, token_grad, keys = finish(sent, incoming, own, *back)
    return (
        keys[None],
        token_grad[None],
        new_params[None],
        new_first[None],
        new_second[None],
        mixed,
    )


def body(*args):
    branches = [partial(step_with, hop=2**level) for level in range(4)]
    return lax.switch(args[-1][0] & 3, branches, *args)


def solution(mesh):
    fine = Mesh(mesh.devices.reshape(8, 2, 2, 2, 4, 2), REPS + GROUP)
    rows = P(REPS, GROUP, None)
    return jax.shard_map(
        body,
        mesh=fine,
        in_specs=(rows, rows, rows, rows, rows, P(REPS), P()),
        out_specs=(rows, rows, rows, rows, rows, P(REPS)),
        check_vma=False,
    )
```

time: 141 us -> 103 us (0.73); the launches traced: 139 us -> 102 us
  blocking collectives: 50.6 us -> 0 us
  starting transfers between devices: 29.4 us -> 45.3 us
  Pallas kernels: 0 us -> 12.2 us
  local copies, waits for them, and re-layouts: 14.4 us -> 2.8 us
  waiting for transfers between devices: 30.3 us -> 38.6 us
  other arithmetic: 5.58 us -> 0.07 us
  matrix products: 4.52 us -> 0 us
  between operations: 3.95 us -> 1.46 us
  loops' own time: 0.02 us -> 1.72 us
    all_to_all x2 -> x0, blocking collectives: 50.6 us -> none  [the longest x1 30.8 us: swap_features(): lax.all_to_all(x, PAIRS, 0, 0, axis_index_groups=feature_groups(), tiled=...]
    ppermute x0 -> x7, waiting for transfers between devices: none -> 28.3 us  [the longest x4 19.7 us: along_quad(): return lax.ppermute(x, 'zq', [(i, (i + step) % 4) for i in range(4)])]
    ppermute x0 -> x7, starting transfers between devices: none -> 25.5 us  [the longest x4 14.5 us: along_quad(): return lax.ppermute(x, 'zq', [(i, (i + step) % 4) for i in range(4)])]
    pallas_call x0 -> x5, Pallas kernels: none -> 12.2 us  [the longest x1 3.65 us: pack(): pl.pallas_call(pack_kernel, grid=(4,), in_specs=[*columns, pl.BlockSpec((...]
    ppermute x1, waiting for transfers between devices: 14.5 us -> 3.25 us  [pushed(): return lax.ppermute(outgoing, REPS, pairs)]
    all_to_all x2, waiting for transfers between devices: 15.8 us -> 7.1 us  [the longest x1 7.1 us: step_with(): shares = lax.all_to_all(share(got), 'zq', 0, 0, tiled=True)]
    all_to_all x2, starting transfers between devices: 23.9 us -> 17 us  [the longest x1 13.4 us: step_with(): lax.all_to_all(out, PAIRS, 0, 0, axis_index_groups=feature_groups(), tile...]
    dot_general x3 -> x0, matrix products: 4.52 us -> none  [the longest x1 3.08 us: body(): lax.dot_general(tok, cot, (((0,), (0,)), ((), ())), preferred_element_typ...]
  transfers between devices with their start and end apart: 3 -> 10, of which waited for: 2 -> 6; matrix products, arithmetic and copies ran while one was open for 3% -> 0% of each run, Pallas kernels for 0% -> 5%
where the time goes in v2:
time: 103 us; the launch traced here: 102 us
  starting transfers between devices  45.3 us (44%)
  waiting for transfers between devices  38.6 us (37%)
  Pallas kernels  12.2 us (12%)
  local copies, waits for them, and re-layouts  2.8 us (3%)
  loops' own time  1.72 us (2%)
  between operations  1.46 us (1%)
    ppermute x4, waiting for transfers between devices, along_quad(): return lax.ppermute(x, 'zq', [(i, (i + step) % 4) for i in range(4)])  19.7 us
    ppermute x4, starting transfers between devices, along_quad(): return lax.ppermute(x, 'zq', [(i, (i + step) % 4) for i in range(4)])  14.5 us
    all_to_all x1, starting transfers between devices, step_with(): lax.all_to_all(out, PAIRS, 0, 0, axis_index_groups=feature_groups(), tile...  13.4 us
    ppermute x3, starting transfers between devices, step_with(): lax.ppermute(x, PAIRS, partner_pairs(r + 1))  11.1 us
    ppermute x3, waiting for transfers between devices, step_with(): lax.ppermute(x, PAIRS, partner_pairs(r + 1))  8.6 us
    all_to_all x1, waiting for transfers between devices, step_with(): shares = lax.all_to_all(share(got), 'zq', 0, 0, tiled=True)  7.1 us
    pallas_call x1, Pallas kernels, pack(): pl.pallas_call(pack_kernel, grid=(4,), in_specs=[*columns, pl.BlockSpec((...  3.65 us
    all_to_all x1, starting transfers between devices, step_with(): shares = lax.all_to_all(share(got), 'zq', 0, 0, tiled=True)  3.53 us
  transfers between devices with their start and end apart: 10, of which 6 were waited for; matrix products, arithmetic and copies ran while one was open for 0% of the time, Pallas kernels for 5%

profile of v2, /device:TPU:1, one launch (start us, length us, event | category | flops | bytes accessed | tf_op | source)
XLA Modules:
  0.0 102.2 jit_solution(2319250380795549182)
XLA Ops:
  1.3 100.8 %conditional.1 = (f32[1]{0:T(128)}, bf16[1,128,512]{2,1,0:T(8,128)(2,1)}, bf16[1,128,4096]{2,1,0:T(8,128)(2,1)}, bf16[1,256,512]{2,1,0:T(8,128)(2,1)}, f32[1,256,512]{2,1,0:T(8,128)}, /*index=5*/f32[1,256,512]{2,1,0:T(8,128)}) conditional(s32[]{:T(128)} %bitcast.52, (bf16[1]{0:T(256)(128)(2,1)}, s32[1]{0:T(128)}, ...), branch_computations={%region_0.0_spmd, %region_1.0_spmd, %region_2.0_spmd, %region_3.0_... | conditional | flops 1611005952 | bytes 41485024 | solution.py:233
  1.3 3.6 %pack.5 = bf16[4,128,1536]{2,1,0:T(8,128)(2,1)} custom-call(bf16[128,4096]{1,0:T(8,128)(2,1)} %bitcast.73, bf16[128,4096]{1,0:T(8,128)(2,1)} %bitcast.74, bf16[128,4096]{1,0:T(8,128)(2,1)} %bitcast.75, bf16[128,4096]{1,0:T(8,128)(2,1)} %bitcast.76, bf16[128,512]{1,0:T(8,128)(2,1)} %bitcast.98), custom_call_target="tpu_custom_call" | custom-call | bytes 3145728 | tf_op jit(solution)/shard_map/cond/branch_1_fun/pack/pallas_call | solution.py:76
  5.0 13.4 %all-to-all-start.2 = ((bf16[4,128,1536]{2,1,0:T(8,128)(2,1)}), bf16[4,128,1536]{2,1,0:T(8,128)(2,1)S(1)}, u32[]{:S(2)}, u32[]{:S(2)}) async-start(bf16[4,128,1536]{2,1,0:T(8,128)(2,1)} %pack.5), calls=%async_computation.2 | async-start | bytes 3145728 | tf_op jit(solution)/shard_map/cond/branch_1_fun/all_to_all | solution.py:206
  19.1 2.2 %collective-permute-start.10 = (bf16[256,512]{1,0:T(8,128)(2,1)S(1)}, bf16[256,512]{1,0:T(8,128)(2,1)S(1)}, u32[]{:S(2)}, u32[]{:S(2)}) collective-permute-start(bf16[256,512]{1,0:T(8,128)(2,1)S(1)} %divide_convert_fusion.1.own_w), channel_id=1, source_target_pairs={{0,6},{2,0},{4,2},{6,4},{1,7},{3,1},{5,3},{7,5},{8,14},{10,8},{12,... | collective-permute-start | bytes 786440 | tf_op jit(solution)/shard_map/cond/branch_1_fun/ppermute | solution.py:46
  21.3 4.0 %collective-permute-start.8 = (bf16[256,512]{1,0:T(8,128)(2,1)S(1)}, bf16[256,512]{1,0:T(8,128)(2,1)S(1)}, u32[]{:S(2)}, u32[]{:S(2)}) collective-permute-start(bf16[256,512]{1,0:T(8,128)(2,1)S(1)} %divide_convert_fusion.1.own_w), channel_id=1, source_target_pairs={{0,2},{2,4},{4,6},{6,0},{1,3},{3,5},{5,7},{7,1},{8,10},{10,12},{12... | collective-permute-start | bytes 786440 | tf_op jit(solution)/shard_map/cond/branch_1_fun/ppermute | solution.py:46
  25.3 13.8 %collective-permute-done.10.w_up = bf16[256,512]{1,0:T(8,128)(2,1)S(1)} collective-permute-done((bf16[256,512]{1,0:T(8,128)(2,1)S(1)}, bf16[256,512]{1,0:T(8,128)(2,1)S(1)}, u32[]{:S(2)}, u32[]{:S(2)}) %collective-permute-start.10) | collective-permute-done | bytes 262176 | tf_op jit(solution)/shard_map/cond/branch_1_fun/ppermute | solution.py:46
  39.1 6.4 %collective-permute-start.11 = (bf16[128,512]{1,0:T(8,128)(2,1)S(1)}, bf16[128,512]{1,0:T(8,128)(2,1)S(1)}, u32[]{:S(2)}, u32[]{:S(2)}) collective-permute-start(bf16[128,512]{1,0:T(8,128)(2,1)S(1)} %slice.27), channel_id=1, source_target_pairs={{0,6},{2,0},{4,2},{6,4},{1,7},{3,1},{5,3},{7,5},{8,14},{10,8},{12,... | collective-permute-start | bytes 393224 | tf_op jit(solution)/shard_map/cond/branch_1_fun/ppermute | solution.py:46
  45.5 0.0 collective-permute-done.8.w_down
  45.5 0.0 copy-start.2
  45.6 1.9 %collective-permute-start.9 = (bf16[128,512]{1,0:T(8,128)(2,1)S(1)}, bf16[128,512]{1,0:T(8,128)(2,1)S(1)}, u32[]{:S(2)}, u32[]{:S(2)}) collective-permute-start(bf16[128,512]{1,0:T(8,128)(2,1)S(1)} %slice.26), channel_id=1, source_target_pairs={{0,2},{2,4},{4,6},{6,0},{1,3},{3,5},{5,7},{7,1},{8,10},{10,12},{12... | collective-permute-start | bytes 393224 | tf_op jit(solution)/shard_map/cond/branch_1_fun/ppermute | solution.py:46
  47.5 0.0 collective-permute-done.11.far_b
  47.5 0.0 copy-start.10
  47.5 5.9 %collective-permute-done.9.far_a = bf16[128,512]{1,0:T(8,128)(2,1)S(1)} collective-permute-done((bf16[128,512]{1,0:T(8,128)(2,1)S(1)}, bf16[128,512]{1,0:T(8,128)(2,1)S(1)}, u32[]{:S(2)}, u32[]{:S(2)}) %collective-permute-start.9) | collective-permute-done | bytes 131104 | tf_op jit(solution)/shard_map/cond/branch_1_fun/ppermute | solution.py:46
  53.4 0.0 all-to-all-done.2
  53.4 2.5 %share.5 = bf16[4,256,512]{2,1,0:T(8,128)(2,1)} custom-call(bf16[512,1536]{1,0:T(8,128)(2,1)S(1)} %bitcast.60, bf16[512,1536]{1,0:T(8,128)(2,1)S(1)} %bitcast.61), custom_call_target="tpu_custom_call" | custom-call | flops 536870912 | bytes 2621440 | tf_op jit(solution)/shard_map/cond/branch_1_fun/share/pallas_call | solution.py:94
  55.9 3.5 %all-to-all-start.3 = ((bf16[4,256,512]{2,1,0:T(8,128)(2,1)}), bf16[4,256,512]{2,1,0:T(8,128)(2,1)S(1)}, u32[]{:S(2)}, u32[]{:S(2)}) async-start(bf16[4,256,512]{2,1,0:T(8,128)(2,1)} %share.5), calls=%async_computation.3 | async-start | bytes 2097152 | tf_op jit(solution)/shard_map/cond/branch_1_fun/all_to_all | solution.py:211
  60.1 0.0 copy-start.3
  60.1 0.9 copy-done.3
  61.0 0.9 copy-done.11
  61.9 0.9 copy-done.19
  62.8 2.3 %products.5 = (bf16[128,1536]{1,0:T(8,128)(2,1)S(1)}, bf16[128,1536]{1,0:T(8,128)(2,1)}, bf16[128,1536]{1,0:T(8,128)(2,1)}, bf16[128,1536]{1,0:T(8,128)(2,1)}) custom-call(bf16[512,1536]{1,0:T(8,128)(2,1)S(1)} %bitcast.62, bf16[256,512]{1,0:T(8,128)(2,1)S(1)} %divide_convert_fusion.1.own_w, bf16[256,512]{1,0:T(8,128)(2,1)S(1)} %copy-done.3, ...), custom_call_target="tpu_custom_call" | custom-call | flops 1073741824 | bytes 4194304 | tf_op jit(solution)/shard_map/cond/branch_1_fun/products/pallas_call | solution.py:126
  65.2 3.9 %collective-permute-start.13 = (bf16[128,1536]{1,0:T(8,128)(2,1)}, bf16[128,1536]{1,0:T(8,128)(2,1)S(1)}, u32[]{:S(2)}, u32[]{:S(2)}) collective-permute-start(bf16[128,1536]{1,0:T(8,128)(2,1)} %get-tuple-element.99), channel_id=1, source_target_pairs={{0,1},{1,0},{2,3},{3,2},{4,5},{5,4},{6,7},{7,6},{8,9},{9,8},{10,11... | collective-permute-start | bytes 1179656 | tf_op jit(solution)/shard_map/cond/branch_1_fun/ppermute | solution.py:214
  69.1 2.7 %collective-permute-start.14 = (bf16[128,1536]{1,0:T(8,128)(2,1)}, bf16[128,1536]{1,0:T(8,128)(2,1)S(1)}, u32[]{:S(2)}, u32[]{:S(2)}) collective-permute-start(bf16[128,1536]{1,0:T(8,128)(2,1)} %get-tuple-element.100), channel_id=1, source_target_pairs={{0,8},{1,9},{2,10},{3,11},{4,12},{5,13},{6,14},{7,15},{8,0},{9,1},... | collective-permute-start | bytes 1179656 | tf_op jit(solution)/shard_map/cond/branch_1_fun/ppermute | solution.py:214
  71.7 4.5 %collective-permute-start.15 = (bf16[128,1536]{1,0:T(8,128)(2,1)}, bf16[128,1536]{1,0:T(8,128)(2,1)S(1)}, u32[]{:S(2)}, u32[]{:S(2)}) collective-permute-start(bf16[128,1536]{1,0:T(8,128)(2,1)} %get-tuple-element.101), channel_id=1, source_target_pairs={{0,9},{1,8},{2,11},{3,10},{4,13},{5,12},{6,15},{7,14},{8,1},{9,0},... | collective-permute-start | bytes 1179656 | tf_op jit(solution)/shard_map/cond/branch_1_fun/ppermute | solution.py:214
  76.3 7.1 %all-to-all-done.3.shares = bf16[4,256,512]{2,1,0:T(8,128)(2,1)S(1)} async-done(((bf16[4,256,512]{2,1,0:T(8,128)(2,1)}), bf16[4,256,512]{2,1,0:T(8,128)(2,1)S(1)}, u32[]{:S(2)}, u32[]{:S(2)}) %all-to-all-start.3) | async-done | bytes 1048608 | tf_op jit(solution)/shard_map/cond/branch_1_fun/all_to_all | solution.py:211
  83.4 2.4 %adam.5 = (f32[256,512]{1,0:T(8,128)}, f32[256,512]{1,0:T(8,128)}, bf16[272,512]{1,0:T(8,128)(2,1)S(1)}) custom-call(f32[1]{0:T(128)} %convert_element_type.45.weight, f32[2]{0:T(128)S(1)} %power_subtract_fusion.1.bias, bf16[4,256,512]{2,1,0:T(8,128)(2,1)S(1)} %all-to-all-done.3.shares, f32[256,512]{1,0:T(8,128)} %bitcast.90, f32[256,512]{1,0:T(8,128)} %bitcast.94, ...), custom_call_target="tpu_custom_call" | custom-call | bytes 4194304 | tf_op jit(solution)/shard_map/cond/branch_1_fun/adam/pallas_call | solution.py:153
  85.9 2.8 %collective-permute-start.12 = (bf16[272,512]{1,0:T(8,128)(2,1)S(1)}, bf16[272,512]{1,0:T(8,128)(2,1)S(1)}, u32[]{:S(2)}, u32[]{:S(2)}) collective-permute-start(bf16[272,512]{1,0:T(8,128)(2,1)S(1)} %get-tuple-element.95.sent), channel_id=1, source_target_pairs={{0,32},{16,48},{32,64},{48,80},{64,96},{80,112},{96,128},{112,144}... | collective-permute-start | bytes 835592 | tf_op jit(solution)/shard_map/cond/branch_1_fun/ppermute | solution.py:51
  88.6 0.9 collective-permute-done.13.from_z
  89.5 0.0 collective-permute-done.14.from_x
  89.5 7.7 %collective-permute-done.15.from_xz = bf16[128,1536]{1,0:T(8,128)(2,1)S(1)} collective-permute-done((bf16[128,1536]{1,0:T(8,128)(2,1)}, bf16[128,1536]{1,0:T(8,128)(2,1)S(1)}, u32[]{:S(2)}, u32[]{:S(2)}) %collective-permute-start.15) | collective-permute-done | bytes 393248 | tf_op jit(solution)/shard_map/cond/branch_1_fun/ppermute | solution.py:214
  97.2 3.3 %collective-permute-done.12.incoming = bf16[272,512]{1,0:T(8,128)(2,1)S(1)} collective-permute-done((bf16[272,512]{1,0:T(8,128)(2,1)S(1)}, bf16[272,512]{1,0:T(8,128)(2,1)S(1)}, u32[]{:S(2)}, u32[]{:S(2)}) %collective-permute-start.12) | collective-permute-done | bytes 278560 | tf_op jit(solution)/shard_map/cond/branch_1_fun/ppermute | solution.py:51
  100.5 1.3 %finish.5 = (bf16[256,512]{1,0:T(8,128)(2,1)}, f32[1]{0:T(128)}, bf16[128,4096]{1,0:T(8,128)(2,1)}, bf16[128,512]{1,0:T(8,128)(2,1)}) custom-call(bf16[272,512]{1,0:T(8,128)(2,1)S(1)} %get-tuple-element.95.sent, bf16[272,512]{1,0:T(8,128)(2,1)S(1)} %collective-permute-done.12.incoming, bf16[128,1536]{1,0:T(8,128)(2,1)S(1)} %get-tuple-element.98.own, ...), custom_call_target="tpu_custom_call" | custom-call | bytes 4194304 | tf_op jit(solution)/shard_map/cond/branch_1_fun/finish/pallas_call | solution.py:181
  (14 shorter events, 0.1 us)
Async XLA Ops:
  5.0 14.1 %copy-start.25 = (bf16[1,256,512]{2,1,0:T(8,128)(2,1)S(1)}, bf16[1,256,512]{2,1,0:T(8,128)(2,1)}, u32[]{:S(2)}) copy-start(bf16[1,256,512]{2,1,0:T(8,128)(2,1)} %get-tuple-element.91) | copy-start | bytes 786436 | tf_op jit(solution)/shard_map/cond
  5.0 48.4 %all-to-all-start.2 = ((bf16[4,128,1536]{2,1,0:T(8,128)(2,1)}), bf16[4,128,1536]{2,1,0:T(8,128)(2,1)S(1)}, u32[]{:S(2)}, u32[]{:S(2)}) async-start(bf16[4,128,1536]{2,1,0:T(8,128)(2,1)} %pack.5), calls=%async_computation.2 | async-start | bytes 3145728 | tf_op jit(solution)/shard_map/cond/branch_1_fun/all_to_all | solution.py:206
  19.1 20.0 %collective-permute-start.10 = (bf16[256,512]{1,0:T(8,128)(2,1)S(1)}, bf16[256,512]{1,0:T(8,128)(2,1)S(1)}, u32[]{:S(2)}, u32[]{:S(2)}) collective-permute-start(bf16[256,512]{1,0:T(8,128)(2,1)S(1)} %divide_convert_fusion.1.own_w), channel_id=1, source_target_pairs={{0,6},{2,0},{4,2},{6,4},{1,7},{3,1},{5,3},{7,5},{8,14},{10,8},{12,... | collective-permute-start | bytes 786440 | tf_op jit(solution)/shard_map/cond/branch_1_fun/ppermute | solution.py:46
  21.3 24.2 %collective-permute-start.8 = (bf16[256,512]{1,0:T(8,128)(2,1)S(1)}, bf16[256,512]{1,0:T(8,128)(2,1)S(1)}, u32[]{:S(2)}, u32[]{:S(2)}) collective-permute-start(bf16[256,512]{1,0:T(8,128)(2,1)S(1)} %divide_convert_fusion.1.own_w), channel_id=1, source_target_pairs={{0,2},{2,4},{4,6},{6,0},{1,3},{3,5},{5,7},{7,1},{8,10},{10,12},{12... | collective-permute-start | bytes 786440 | tf_op jit(solution)/shard_map/cond/branch_1_fun/ppermute | solution.py:46
  39.1 8.3 %collective-permute-start.11 = (bf16[128,512]{1,0:T(8,128)(2,1)S(1)}, bf16[128,512]{1,0:T(8,128)(2,1)S(1)}, u32[]{:S(2)}, u32[]{:S(2)}) collective-permute-start(bf16[128,512]{1,0:T(8,128)(2,1)S(1)} %slice.27), channel_id=1, source_target_pairs={{0,6},{2,0},{4,2},{6,4},{1,7},{3,1},{5,3},{7,5},{8,14},{10,8},{12,... | collective-permute-start | bytes 393224 | tf_op jit(solution)/shard_map/cond/branch_1_fun/ppermute | solution.py:46
  45.5 10.4 %copy-start.2 = (bf16[256,512]{1,0:T(8,128)(2,1)}, bf16[256,512]{1,0:T(8,128)(2,1)S(1)}, u32[]{:S(2)}) copy-start(bf16[256,512]{1,0:T(8,128)(2,1)S(1)} %collective-permute-done.8.w_down) | copy-start | bytes 786436 | tf_op jit(solution)/shard_map/cond
  45.6 7.8 %collective-permute-start.9 = (bf16[128,512]{1,0:T(8,128)(2,1)S(1)}, bf16[128,512]{1,0:T(8,128)(2,1)S(1)}, u32[]{:S(2)}, u32[]{:S(2)}) collective-permute-start(bf16[128,512]{1,0:T(8,128)(2,1)S(1)} %slice.26), channel_id=1, source_target_pairs={{0,2},{2,4},{4,6},{6,0},{1,3},{3,5},{5,7},{7,1},{8,10},{10,12},{12... | collective-permute-start | bytes 393224 | tf_op jit(solution)/shard_map/cond/branch_1_fun/ppermute | solution.py:46
  47.5 8.4 %copy-start.10 = (bf16[128,512]{1,0:T(8,128)(2,1)}, bf16[128,512]{1,0:T(8,128)(2,1)S(1)}, u32[]{:S(2)}) copy-start(bf16[128,512]{1,0:T(8,128)(2,1)S(1)} %collective-permute-done.11.far_b) | copy-start | bytes 393220 | tf_op jit(solution)/shard_map/cond
  53.4 2.5 %copy-start.18 = (bf16[128,512]{1,0:T(8,128)(2,1)}, bf16[128,512]{1,0:T(8,128)(2,1)S(1)}, u32[]{:S(2)}) copy-start(bf16[128,512]{1,0:T(8,128)(2,1)S(1)} %collective-permute-done.9.far_a) | copy-start | bytes 393220 | tf_op jit(solution)/shard_map/cond
  55.9 27.5 %all-to-all-start.3 = ((bf16[4,256,512]{2,1,0:T(8,128)(2,1)}), bf16[4,256,512]{2,1,0:T(8,128)(2,1)S(1)}, u32[]{:S(2)}, u32[]{:S(2)}) async-start(bf16[4,256,512]{2,1,0:T(8,128)(2,1)} %share.5), calls=%async_computation.3 | async-start | bytes 2097152 | tf_op jit(solution)/shard_map/cond/branch_1_fun/all_to_all | solution.py:211
  60.1 1.0 copy-start.3
  61.0 0.9 copy-start.11
  61.9 0.9 copy-start.19
  62.8 13.4 %copy-start.29 = (f32[2]{0:T(128)S(1)}, f32[2]{0:T(128)}, u32[]{:S(2)}) copy-start(f32[2]{0:T(128)} %get-tuple-element.87) | copy-start | bytes 28 | tf_op jit(solution)/shard_map/cond
  65.2 24.4 %collective-permute-start.13 = (bf16[128,1536]{1,0:T(8,128)(2,1)}, bf16[128,1536]{1,0:T(8,128)(2,1)S(1)}, u32[]{:S(2)}, u32[]{:S(2)}) collective-permute-start(bf16[128,1536]{1,0:T(8,128)(2,1)} %get-tuple-element.99), channel_id=1, source_target_pairs={{0,1},{1,0},{2,3},{3,2},{4,5},{5,4},{6,7},{7,6},{8,9},{9,8},{10,11... | collective-permute-start | bytes 1179656 | tf_op jit(solution)/shard_map/cond/branch_1_fun/ppermute | solution.py:214
  69.1 20.5 %collective-permute-start.14 = (bf16[128,1536]{1,0:T(8,128)(2,1)}, bf16[128,1536]{1,0:T(8,128)(2,1)S(1)}, u32[]{:S(2)}, u32[]{:S(2)}) collective-permute-start(bf16[128,1536]{1,0:T(8,128)(2,1)} %get-tuple-element.100), channel_id=1, source_target_pairs={{0,8},{1,9},{2,10},{3,11},{4,12},{5,13},{6,14},{7,15},{8,0},{9,1},... | collective-permute-start | bytes 1179656 | tf_op jit(solution)/shard_map/cond/branch_1_fun/ppermute | solution.py:214
  71.7 25.5 %collective-permute-start.15 = (bf16[128,1536]{1,0:T(8,128)(2,1)}, bf16[128,1536]{1,0:T(8,128)(2,1)S(1)}, u32[]{:S(2)}, u32[]{:S(2)}) collective-permute-start(bf16[128,1536]{1,0:T(8,128)(2,1)} %get-tuple-element.101), channel_id=1, source_target_pairs={{0,9},{1,8},{2,11},{3,10},{4,13},{5,12},{6,15},{7,14},{8,1},{9,0},... | collective-permute-start | bytes 1179656 | tf_op jit(solution)/shard_map/cond/branch_1_fun/ppermute | solution.py:214
  85.9 14.6 %collective-permute-start.12 = (bf16[272,512]{1,0:T(8,128)(2,1)S(1)}, bf16[272,512]{1,0:T(8,128)(2,1)S(1)}, u32[]{:S(2)}, u32[]{:S(2)}) collective-permute-start(bf16[272,512]{1,0:T(8,128)(2,1)S(1)} %get-tuple-element.95.sent), channel_id=1, source_target_pairs={{0,32},{16,48},{32,64},{48,80},{64,96},{80,112},{96,128},{112,144}... | collective-permute-start | bytes 835592 | tf_op jit(solution)/shard_map/cond/branch_1_fun/ppermute | solution.py:51

commit v3 on v2

v3 whole, which is shorter than its diff:
```python
from functools import partial

import jax
import jax.numpy as jnp
from jax import lax
from jax.experimental import pallas as pl
from jax.experimental.pallas import tpu as pltpu
from jax.sharding import Mesh, PartitionSpec as P

LEARN = 0.002
BETA_ONE = 0.9
BETA_TWO = 0.999
EPSILON = 1e-08
GROUP = ("xh", "zq", "zp")
REPS = ("y", "xl", "c")
PAIRS = ("c", "xh", "zq", "zp")
SHARE = 64 << 20
ADAM = 64 << 20
COMBINE = 64 << 20
F32 = jnp.float32
BF16 = jnp.bfloat16


def neighbour(core, z):
    return z ^ 1 if core == 0 else ((z + 1) ^ 1) - 1 & 7


def partner_pairs(relative):
    pairs = []
    for core in range(2):
        for xh in range(2):
            for z in range(8):
                to_z = neighbour(core, z) if relative & 1 else z
                to_x = xh ^ (relative >> 1)
                pairs.append((core * 16 + xh * 8 + z, core * 16 + to_x * 8 + to_z))
    return pairs


def along_quad(x, step):
    return lax.ppermute(x, "zq", [(i, (i + step) % 4) for i in range(4)])


def swap_tokens(x):
    return lax.all_to_all(x, "zq", 0, 0, tiled=True)


def swap_features(x, relative):
    return lax.ppermute(x, PAIRS, partner_pairs(relative))


def pushed(outgoing, hop):
    pairs = [(source, (source + hop) % 32) for source in range(32)]
    return lax.ppermute(outgoing, REPS, pairs)


VMEM = pl.BlockSpec(memory_space=pltpu.VMEM)
ANY = pl.BlockSpec(memory_space=pl.ANY)
SMEM = pl.BlockSpec(memory_space=pltpu.SMEM)


def params_of(flops=0, moved=0, mib=48):
    return dict(
        compiler_params=pltpu.CompilerParams(vmem_limit_bytes=mib << 20),
        cost_estimate=pl.CostEstimate(flops=flops, bytes_accessed=moved, transcendentals=0),
    )


def pack_kernel(tokens, cot, own, to_z, to_x, to_xz):
    place = lax.axis_index("xh") * 2 + lax.axis_index("zp")
    for relative, out in enumerate((own, to_z, to_x, to_xz)):
        cls = place ^ relative
        for q in range(4):
            column = (cls // 2) * 2048 + q * 512 + (cls % 2) * 256
            out[:, q * 256 : (q + 1) * 256] = tokens[:, pl.ds(pl.multiple_of(column, 256), 256)]
        out[:, 1024:] = cot[...]


def pack(tokens, cot):
    return pl.pallas_call(
        pack_kernel,
        in_specs=[VMEM] * 2,
        out_specs=[VMEM] * 4,
        out_shape=[jax.ShapeDtypeStruct((128, 1536), BF16)] * 4,
        name="pack",
        **params_of(0, 3 << 20),
    )(tokens, cot)


def share_kernel(t0, t1, t2, t3, c0, c1, c2, c3, out):
    total = None
    for tok, cot in ((t0, c0), (t1, c1), (t2, c2), (t3, c3)):
        term = lax.dot_general(
            tok[...], cot[...], (((0,), (0,)), ((), ())), preferred_element_type=F32
        )
        total = term if total is None else total + term
    out[0] = total.astype(BF16)


def share(blocks):
    return pl.pallas_call(
        share_kernel,
        grid=(4,),
        in_specs=[pl.BlockSpec((128, 256), lambda q: (0, q))] * 4
        + [pl.BlockSpec((128, 512), lambda q: (0, 2))] * 4,
        out_specs=pl.BlockSpec((1, 256, 512), lambda q: (q, 0, 0)),
        out_shape=pltpu.HBM((4, 256, 512), BF16),
        name="share",
        **params_of(0, SHARE),
    )(*blocks, *blocks)


def product_kernel(b0, b1, b2, b3, w0, w1, w2, w3, own, to_z, to_x, to_xz, got):
    quad = lax.axis_index("zq")
    for k, block in enumerate((b0, b1, b2, b3)):
        got[k * 128 : (k + 1) * 128, :] = block[...]
    outs = (own, to_z, to_x, to_xz)
    cot = got[:, 1024:]
    keys = None
    for q, w in enumerate((w0, w1, w2, w3)):
        columns = pl.ds(pl.multiple_of(lax.rem(quad + q, 4) * 256, 256), 256)
        term = jnp.dot(got[:, columns], w[...], preferred_element_type=F32)
        keys = term if keys is None else keys + term
        part = lax.dot_general(
            cot, w[...], (((1,), (1,)), ((), ())), preferred_element_type=F32
        ).astype(BF16)
        for k, out in enumerate(outs):
            out[:, columns] = part[k * 128 : (k + 1) * 128, :]
    keys = keys.astype(BF16)
    for k, out in enumerate(outs):
        out[:, 1024:] = keys[k * 128 : (k + 1) * 128, :]


def products(blocks, w):
    block = jax.ShapeDtypeStruct((128, 1536), BF16)
    return pl.pallas_call(
        product_kernel,
        in_specs=[VMEM] * 8,
        out_specs=[VMEM] * 4,
        out_shape=[block] * 4,
        scratch_shapes=[pltpu.VMEM((512, 1536), BF16)],
        name="products",
        **params_of(4 * 512 * 1024 * 512, 4 << 20),
    )(*blocks, *w)


def adam_kernel(weight, bias, shares, first, second, numer, new_first, new_second, sent):
    total = shares[0].astype(F32)
    for q in range(1, 4):
        total = total + shares[q].astype(F32)
    grad = total / 2048.0
    one = BETA_ONE * first[...] + (1.0 - BETA_ONE) * grad
    two = BETA_TWO * second[...] + (1.0 - BETA_TWO) * grad * grad
    new_first[...] = one
    new_second[...] = two
    update = LEARN * (one / bias[0]) / (jnp.sqrt(two / bias[1]) + EPSILON)
    sent[:256, :] = (numer[...].astype(F32) - update).astype(BF16)
    sent[256:, :] = jnp.full((16, 512), weight[0], F32).astype(BF16)


def adam(weight, bias, shares, first, second, numer):
    state = jax.ShapeDtypeStruct((256, 512), F32)
    return pl.pallas_call(
        adam_kernel,
        in_specs=[SMEM, SMEM] + [VMEM] * 4,
        out_specs=[VMEM] * 3,
        out_shape=[state, state, jax.ShapeDtypeStruct((272, 512), BF16)],
        name="adam",
        **params_of(0, ADAM),
    )(weight, bias, shares, first, second, numer)


def combine_kernel(sent, incoming, new_params, mixed):
    new_params[...] = (
        (sent[:256, :].astype(F32) + incoming[:256, :].astype(F32)) * 0.5
    ).astype(BF16)
    mixed[0] = (
        jnp.max(sent[256:264, :128].astype(F32)) + jnp.max(incoming[256:264, :128].astype(F32))
    ) * 0.5


def combine(sent, incoming):
    return pl.pallas_call(
        combine_kernel,
        in_specs=[VMEM] * 2,
        out_specs=[VMEM, SMEM],
        out_shape=[jax.ShapeDtypeStruct((256, 512), BF16), jax.ShapeDtypeStruct((1,), F32)],
        name="combine",
        **params_of(0, COMBINE),
    )(sent, incoming)


def unpack_kernel(own, from_z, from_x, from_xz, token_grad, keys):
    place = lax.axis_index("xh") * 2 + lax.axis_index("zp")
    total = None
    for relative, part in enumerate((own, from_z, from_x, from_xz)):
        cls = place ^ relative
        for q in range(4):
            column = (cls // 2) * 2048 + q * 512 + (cls % 2) * 256
            token_grad[:, pl.ds(pl.multiple_of(column, 256), 256)] = part[:, q * 256 : (q + 1) * 256]
        term = part[:, 1024:].astype(F32)
        total = term if total is None else total + term
    keys[...] = total.astype(BF16)


def unpack(own, from_z, from_x, from_xz):
    return pl.pallas_call(
        unpack_kernel,
        in_specs=[VMEM] * 4,
        out_specs=[VMEM] * 2,
        out_shape=[jax.ShapeDtypeStruct((128, 4096), BF16), jax.ShapeDtypeStruct((128, 512), BF16)],
        name="unpack",
        **params_of(0, 3 << 20),
    )(own, from_z, from_x, from_xz)


def step_with(tokens, cotangent, params, first_moment, second_moment, weight, step, hop):
    mass = weight.astype(F32)
    tstep = step[0]
    count = (tstep + 1).astype(F32)
    bias = 1.0 - jnp.power(jnp.array([BETA_ONE, BETA_TWO], F32), count)

    debiased = (params[0].astype(F32) / mass[0]).astype(BF16)
    w_down = along_quad(debiased, 1)
    w_up = along_quad(debiased, -1)
    far = jnp.concatenate([along_quad(w_down[:128], 1), along_quad(w_up[128:], -1)], axis=0)
    rows = [debiased, w_up, far, w_down]
    own, *sends = pack(tokens[0], cotangent[0])
    blocks = [own] + [swap_features(x, r + 1) for r, x in enumerate(sends)]
    rows, blocks = lax.optimization_barrier((rows, blocks))
    shares = swap_tokens(share(blocks))

    own, *sends = products(blocks, rows)
    back = [swap_features(x, r + 1) for r, x in enumerate(sends)]

    new_first, new_second, sent = adam(
        mass, bias, shares, first_moment[0], second_moment[0], params[0]
    )
    incoming = pushed(sent, hop)
    new_params, mixed = combine(sent, incoming)
    token_grad, keys = unpack(own, *back)
    return (
        keys[None],
        token_grad[None],
        new_params[None],
        new_first[None],
        new_second[None],
        mixed,
    )


def body(*args):
    branches = [partial(step_with, hop=2**level) for level in range(4)]
    return lax.switch(args[-1][0] & 3, branches, *args)


def solution(mesh):
    fine = Mesh(mesh.devices.reshape(8, 2, 2, 2, 4, 2), REPS + GROUP)
    rows = P(REPS, GROUP, None)
    return jax.shard_map(
        body,
        mesh=fine,
        in_specs=(rows, rows, rows, rows, rows, P(REPS), P()),
        out_specs=(rows, rows, rows, rows, rows, P(REPS)),
        check_vma=False,
    )
```

time: 103 us -> 94.5 us (0.917)
  waiting for transfers between devices: 38.6 us -> 25.4 us
  starting transfers between devices: 45.3 us -> 50.5 us
  Pallas kernels: 12.2 us -> 11 us
    all_to_all x2 -> x1, starting transfers between devices: 17 us -> 4.34 us  [swap_tokens(): return lax.all_to_all(x, 'zq', 0, 0, tiled=True)]
    ppermute x4, waiting for transfers between devices: 19.7 us -> 8.2 us  [along_quad(): return lax.ppermute(x, 'zq', [(i, (i + step) % 4) for i in range(4)])]
    ppermute x3 -> x6, starting transfers between devices: 11.1 us -> 22.2 us  [swap_features(): return lax.ppermute(x, PAIRS, partner_pairs(relative))]
    ppermute x4, starting transfers between devices: 14.5 us -> 20.8 us  [along_quad(): return lax.ppermute(x, 'zq', [(i, (i + step) % 4) for i in range(4)])]
    ppermute x3 -> x6, waiting for transfers between devices: 8.6 us -> 5.5 us  [swap_features(): return lax.ppermute(x, PAIRS, partner_pairs(relative))]
    all_to_all x2 -> x1, waiting for transfers between devices: 7.1 us -> 9.98 us  [swap_tokens(): return lax.all_to_all(x, 'zq', 0, 0, tiled=True)]
    ppermute x1, waiting for transfers between devices: 3.25 us -> 1.71 us  [pushed(): return lax.ppermute(outgoing, REPS, pairs)]
    pallas_call x4 -> x5, Pallas kernels: 9.8 us -> 8.58 us  [the longest x1 2.94 us: share(): pl.pallas_call(share_kernel, grid=(4,), in_specs=[pl.BlockSpec((128, 256)...]
  transfers between devices with their start and end apart: 10 -> 12, of which waited for: 6 -> 5; matrix products, arithmetic and copies ran while one was open for 0% -> 0% of each run, Pallas kernels for 5% -> 8%
where the time goes in v3:
time: 94.5 us; the launch traced here: 93.8 us
  starting transfers between devices  50.5 us (53%)
  waiting for transfers between devices  25.4 us (27%)
  Pallas kernels  11 us (12%)
  local copies, waits for them, and re-layouts  2.59 us (3%)
  loops' own time  1.78 us (2%)
  between operations  1.47 us (2%)
  other arithmetic  1.07 us (1%)
    ppermute x6, starting transfers between devices, swap_features(): return lax.ppermute(x, PAIRS, partner_pairs(relative))  22.2 us
    ppermute x4, starting transfers between devices, along_quad(): return lax.ppermute(x, 'zq', [(i, (i + step) % 4) for i in range(4)])  20.8 us
    all_to_all x1, waiting for transfers between devices, swap_tokens(): return lax.all_to_all(x, 'zq', 0, 0, tiled=True)  9.98 us
    ppermute x4, waiting for transfers between devices, along_quad(): return lax.ppermute(x, 'zq', [(i, (i + step) % 4) for i in range(4)])  8.2 us
    ppermute x6, waiting for transfers between devices, swap_features(): return lax.ppermute(x, PAIRS, partner_pairs(relative))  5.5 us
    all_to_all x1, starting transfers between devices, swap_tokens(): return lax.all_to_all(x, 'zq', 0, 0, tiled=True)  4.34 us
    ppermute x1, starting transfers between devices, pushed(): return lax.ppermute(outgoing, REPS, pairs)  3.19 us
    pallas_call x1, Pallas kernels, share(): pl.pallas_call(share_kernel, grid=(4,), in_specs=[pl.BlockSpec((128, 256)...  2.94 us
  transfers between devices with their start and end apart: 12, of which 5 were waited for; matrix products, arithmetic and copies ran while one was open for 0% of the time, Pallas kernels for 8%

profile of v3, /device:TPU:1, one launch (start us, length us, event | category | flops | bytes accessed | tf_op | source)
XLA Modules:
  0.0 93.8 jit_solution(4576755268605277756)
XLA Ops:
  1.3 0.0 copy-start.20
  1.3 0.6 copy-done.20
  1.9 91.7 %conditional.1 = (f32[1]{0:T(128)}, bf16[1,128,512]{2,1,0:T(8,128)(2,1)}, bf16[1,128,4096]{2,1,0:T(8,128)(2,1)}, bf16[1,256,512]{2,1,0:T(8,128)(2,1)}, f32[1,256,512]{2,1,0:T(8,128)}, /*index=5*/f32[1,256,512]{2,1,0:T(8,128)}) conditional(s32[]{:T(128)} %bitcast.48, (bf16[1,256,512]{2,1,0:T(8,128)(2,1)}, ...), branch_computations={%region_0.0_spmd, %region_1.0_spmd, %region_2.0_spmd, %region_3.0_... | conditional | flops 1074659328 | bytes 234947216 | solution.py:253
  2.6 0.0 copy-start.18
  2.6 1.0 %divide_convert_fusion.2.w0 = bf16[256,512]{1,0:T(8,128)(2,1)S(1)} fusion(f32[]{:T(128)} %bitcast.26, bf16[1,256,512]{2,1,0:T(8,128)(2,1)} %get-tuple-element.126), kind=kLoop, calls=%fused_computation.6 | loop fusion | flops 393216 | bytes 524292 | tf_op jit(solution)/shard_map/cond/branch_2_fun/convert_element_type | solution.py:222
  3.6 6.6 %collective-permute-start.23 = (bf16[256,512]{1,0:T(8,128)(2,1)S(1)}, bf16[256,512]{1,0:T(8,128)(2,1)S(1)}, u32[]{:S(2)}, u32[]{:S(2)}) collective-permute-start(bf16[256,512]{1,0:T(8,128)(2,1)S(1)} %divide_convert_fusion.2.w0), channel_id=1, source_target_pairs={{0,2},{2,4},{4,6},{6,0},{1,3},{3,5},{5,7},{7,1},{8,10},{10,12},{12... | collective-permute-start | bytes 786440 | tf_op jit(solution)/shard_map/cond/branch_2_fun/ppermute | solution.py:40
  10.3 6.8 %collective-permute-start.22 = (bf16[256,512]{1,0:T(8,128)(2,1)S(1)}, bf16[256,512]{1,0:T(8,128)(2,1)S(1)}, u32[]{:S(2)}, u32[]{:S(2)}) collective-permute-start(bf16[256,512]{1,0:T(8,128)(2,1)S(1)} %divide_convert_fusion.2.w0), channel_id=1, source_target_pairs={{0,6},{2,0},{4,2},{6,4},{1,7},{3,1},{5,3},{7,5},{8,14},{10,8},{12,... | collective-permute-start | bytes 786440 | tf_op jit(solution)/shard_map/cond/branch_2_fun/ppermute | solution.py:40
  17.1 1.4 %pack.6 = (bf16[128,1536]{1,0:T(8,128)(2,1)S(1)}, bf16[128,1536]{1,0:T(8,128)(2,1)S(1)}, bf16[128,1536]{1,0:T(8,128)(2,1)S(1)}, bf16[128,1536]{1,0:T(8,128)(2,1)S(1)}) custom-call(bf16[128,4096]{1,0:T(8,128)(2,1)} %bitcast.59, bf16[128,512]{1,0:T(8,128)(2,1)S(1)} %bitcast.71), custom_call_target="tpu_custom_call" | custom-call | bytes 3145728 | tf_op jit(solution)/shard_map/cond/branch_2_fun/pack/pallas_call | solution.py:79
  18.5 4.3 %collective-permute-start.26 = (bf16[128,1536]{1,0:T(8,128)(2,1)S(1)}, bf16[128,1536]{1,0:T(8,128)(2,1)S(1)}, u32[]{:S(2)}, u32[]{:S(2)}) collective-permute-start(bf16[128,1536]{1,0:T(8,128)(2,1)S(1)} %get-tuple-element.131), channel_id=1, source_target_pairs={{0,1},{1,0},{2,3},{3,2},{4,5},{5,4},{6,7},{7,6},{8,9},{9,8},{10,11... | collective-permute-start | bytes 1179656 | tf_op jit(solution)/shard_map/cond/branch_2_fun/ppermute | solution.py:48
  22.7 4.7 %collective-permute-start.27 = (bf16[128,1536]{1,0:T(8,128)(2,1)S(1)}, bf16[128,1536]{1,0:T(8,128)(2,1)S(1)}, u32[]{:S(2)}, u32[]{:S(2)}) collective-permute-start(bf16[128,1536]{1,0:T(8,128)(2,1)S(1)} %get-tuple-element.132), channel_id=1, source_target_pairs={{0,8},{1,9},{2,10},{3,11},{4,12},{5,13},{6,14},{7,15},{8,0},{9,1},... | collective-permute-start | bytes 1179656 | tf_op jit(solution)/shard_map/cond/branch_2_fun/ppermute | solution.py:48
  27.4 2.2 %collective-permute-start.28 = (bf16[128,1536]{1,0:T(8,128)(2,1)S(1)}, bf16[128,1536]{1,0:T(8,128)(2,1)S(1)}, u32[]{:S(2)}, u32[]{:S(2)}) collective-permute-start(bf16[128,1536]{1,0:T(8,128)(2,1)S(1)} %get-tuple-element.133), channel_id=1, source_target_pairs={{0,9},{1,8},{2,11},{3,10},{4,13},{5,12},{6,15},{7,14},{8,1},{9,0},... | collective-permute-start | bytes 1179656 | tf_op jit(solution)/shard_map/cond/branch_2_fun/ppermute | solution.py:48
  29.6 0.0 copy-start.4
  29.6 1.9 %collective-permute-start.24 = (bf16[128,512]{1,0:T(8,128)(2,1)S(1)}, bf16[128,512]{1,0:T(8,128)(2,1)S(1)}, u32[]{:S(2)}, u32[]{:S(2)}) collective-permute-start(bf16[128,512]{1,0:T(8,128)(2,1)S(1)} %slice.28), channel_id=1, source_target_pairs={{0,2},{2,4},{4,6},{6,0},{1,3},{3,5},{5,7},{7,1},{8,10},{10,12},{12... | collective-permute-start | bytes 393224 | tf_op jit(solution)/shard_map/cond/branch_2_fun/ppermute | solution.py:40
  31.6 0.0 copy-start.12
  31.6 5.5 %collective-permute-start.25 = (bf16[128,512]{1,0:T(8,128)(2,1)S(1)}, bf16[128,512]{1,0:T(8,128)(2,1)S(1)}, u32[]{:S(2)}, u32[]{:S(2)}) collective-permute-start(bf16[128,512]{1,0:T(8,128)(2,1)S(1)} %slice.29), channel_id=1, source_target_pairs={{0,6},{2,0},{4,2},{6,4},{1,7},{3,1},{5,3},{7,5},{8,14},{10,8},{12,... | collective-permute-start | bytes 393224 | tf_op jit(solution)/shard_map/cond/branch_2_fun/ppermute | solution.py:40
  37.1 2.4 %collective-permute-done.24 = bf16[128,512]{1,0:T(8,128)(2,1)S(1)} collective-permute-done((bf16[128,512]{1,0:T(8,128)(2,1)S(1)}, bf16[128,512]{1,0:T(8,128)(2,1)S(1)}, u32[]{:S(2)}, u32[]{:S(2)}) %collective-permute-start.24) | collective-permute-done | bytes 131104 | tf_op jit(solution)/shard_map/cond/branch_2_fun/ppermute | solution.py:40
  39.5 5.8 %collective-permute-done.25 = bf16[128,512]{1,0:T(8,128)(2,1)S(1)} collective-permute-done((bf16[128,512]{1,0:T(8,128)(2,1)S(1)}, bf16[128,512]{1,0:T(8,128)(2,1)S(1)}, u32[]{:S(2)}, u32[]{:S(2)}) %collective-permute-start.25) | collective-permute-done | bytes 131104 | tf_op jit(solution)/shard_map/cond/branch_2_fun/ppermute | solution.py:40
  45.3 2.9 %share.6 = bf16[4,256,512]{2,1,0:T(8,128)(2,1)} custom-call(bf16[128,1536]{1,0:T(8,128)(2,1)S(1)} %get-tuple-element.134.b0.t0.c0, bf16[128,1536]{1,0:T(8,128)(2,1)S(1)} %collective-permute-done.26.b1.t1.c1, bf16[128,1536]{1,0:T(8,128)(2,1)S(1)} %collective-permute-done.27.b2.t2.c2, bf16[128,1536]{1,0:T(8,128)(2,1)S(1)} %collective-permute-done.28.b3.t3.c3, ...), custom_call_target="tpu_custom_call" | custom-call | bytes 67108864 | tf_op jit(solution)/shard_map/cond/branch_2_fun/share/pallas_call | solution.py:100
  48.3 4.3 %all-to-all-start.2 = ((bf16[4,256,512]{2,1,0:T(8,128)(2,1)}), bf16[4,256,512]{2,1,0:T(8,128)(2,1)S(1)}, u32[]{:S(2)}, u32[]{:S(2)}) async-start(bf16[4,256,512]{2,1,0:T(8,128)(2,1)} %share.6), calls=%async_computation.2 | async-start | bytes 2097152 | tf_op jit(solution)/shard_map/cond/branch_2_fun/all_to_all | solution.py:44
  53.3 0.9 %copy-done.5 = bf16[256,512]{1,0:T(8,128)(2,1)S(1)} copy-done((bf16[256,512]{1,0:T(8,128)(2,1)S(1)}, bf16[256,512]{1,0:T(8,128)(2,1)}, u32[]{:S(2)}) %copy-start.5) | copy-done | bytes 262168 | tf_op jit(solution)/shard_map/cond
  54.2 0.9 %copy-done.13 = bf16[256,512]{1,0:T(8,128)(2,1)S(1)} copy-done((bf16[256,512]{1,0:T(8,128)(2,1)S(1)}, bf16[256,512]{1,0:T(8,128)(2,1)}, u32[]{:S(2)}) %copy-start.13) | copy-done | bytes 262168 | tf_op jit(solution)/shard_map/cond
  55.2 2.3 %products.6 = (bf16[128,1536]{1,0:T(8,128)(2,1)S(1)}, bf16[128,1536]{1,0:T(8,128)(2,1)}, bf16[128,1536]{1,0:T(8,128)(2,1)}, bf16[128,1536]{1,0:T(8,128)(2,1)}) custom-call(bf16[128,1536]{1,0:T(8,128)(2,1)S(1)} %get-tuple-element.134.b0.t0.c0, bf16[128,1536]{1,0:T(8,128)(2,1)S(1)} %collective-permute-done.26.b1.t1.c1, ...), custom_call_target="tpu_custom_call" | custom-call | flops 1073741824 | bytes 4194304 | tf_op jit(solution)/shard_map/cond/branch_2_fun/products/pallas_call | solution.py:135
  57.5 4.3 %collective-permute-start.29 = (bf16[128,1536]{1,0:T(8,128)(2,1)}, bf16[128,1536]{1,0:T(8,128)(2,1)S(1)}, u32[]{:S(2)}, u32[]{:S(2)}) collective-permute-start(bf16[128,1536]{1,0:T(8,128)(2,1)} %get-tuple-element.143), channel_id=1, source_target_pairs={{0,1},{1,0},{2,3},{3,2},{4,5},{5,4},{6,7},{7,6},{8,9},{9,8},{10,11... | collective-permute-start | bytes 1179656 | tf_op jit(solution)/shard_map/cond/branch_2_fun/ppermute | solution.py:48
  61.8 2.9 %collective-permute-start.30 = (bf16[128,1536]{1,0:T(8,128)(2,1)}, bf16[128,1536]{1,0:T(8,128)(2,1)S(1)}, u32[]{:S(2)}, u32[]{:S(2)}) collective-permute-start(bf16[128,1536]{1,0:T(8,128)(2,1)} %get-tuple-element.144), channel_id=1, source_target_pairs={{0,8},{1,9},{2,10},{3,11},{4,12},{5,13},{6,14},{7,15},{8,0},{9,1},... | collective-permute-start | bytes 1179656 | tf_op jit(solution)/shard_map/cond/branch_2_fun/ppermute | solution.py:48
  64.7 3.8 %collective-permute-start.31 = (bf16[128,1536]{1,0:T(8,128)(2,1)}, bf16[128,1536]{1,0:T(8,128)(2,1)S(1)}, u32[]{:S(2)}, u32[]{:S(2)}) collective-permute-start(bf16[128,1536]{1,0:T(8,128)(2,1)} %get-tuple-element.145), channel_id=1, source_target_pairs={{0,9},{1,8},{2,11},{3,10},{4,13},{5,12},{6,15},{7,14},{8,1},{9,0},... | collective-permute-start | bytes 1179656 | tf_op jit(solution)/shard_map/cond/branch_2_fun/ppermute | solution.py:48
  68.6 10.0 %all-to-all-done.2.shares = bf16[4,256,512]{2,1,0:T(8,128)(2,1)S(1)} async-done(((bf16[4,256,512]{2,1,0:T(8,128)(2,1)}), bf16[4,256,512]{2,1,0:T(8,128)(2,1)S(1)}, u32[]{:S(2)}, u32[]{:S(2)}) %all-to-all-start.2) | async-done | bytes 1048608 | tf_op jit(solution)/shard_map/cond/branch_2_fun/all_to_all | solution.py:44
  78.6 2.4 %adam.6 = (f32[256,512]{1,0:T(8,128)}, f32[256,512]{1,0:T(8,128)}, bf16[272,512]{1,0:T(8,128)(2,1)S(1)}) custom-call(f32[1]{0:T(128)} %convert_element_type.51.weight, f32[2]{0:T(128)S(1)} %power_subtract_fusion.2.bias, bf16[4,256,512]{2,1,0:T(8,128)(2,1)S(1)} %all-to-all-done.2.shares, f32[256,512]{1,0:T(8,128)} %bitcast.63, f32[256,512]{1,0:T(8,128)} %bitcast.67, ...), custom_call_target="tpu_custom_call" | custom-call | bytes 67108864 | tf_op jit(solution)/shard_map/cond/branch_2_fun/adam/pallas_call | solution.py:162
  81.0 3.2 %collective-permute-start.32 = (bf16[272,512]{1,0:T(8,128)(2,1)S(1)}, bf16[272,512]{1,0:T(8,128)(2,1)S(1)}, u32[]{:S(2)}, u32[]{:S(2)}) collective-permute-start(bf16[272,512]{1,0:T(8,128)(2,1)S(1)} %get-tuple-element.152.sent), channel_id=1, source_target_pairs={{0,64},{16,80},{32,96},{48,112},{64,128},{80,144},{96,160},{112,17... | collective-permute-start | bytes 835592 | tf_op jit(solution)/shard_map/cond/branch_2_fun/ppermute | solution.py:53
  84.2 5.5 %collective-permute-done.31.from_xz = bf16[128,1536]{1,0:T(8,128)(2,1)S(1)} collective-permute-done((bf16[128,1536]{1,0:T(8,128)(2,1)}, bf16[128,1536]{1,0:T(8,128)(2,1)S(1)}, u32[]{:S(2)}, u32[]{:S(2)}) %collective-permute-start.31) | collective-permute-done | bytes 393248 | tf_op jit(solution)/shard_map/cond/branch_2_fun/ppermute | solution.py:48
  89.7 1.1 %unpack.6 = (bf16[128,4096]{1,0:T(8,128)(2,1)}, bf16[128,512]{1,0:T(8,128)(2,1)}) custom-call(bf16[128,1536]{1,0:T(8,128)(2,1)S(1)} %get-tuple-element.142.own, bf16[128,1536]{1,0:T(8,128)(2,1)S(1)} %collective-permute-done.29.from_z, bf16[128,1536]{1,0:T(8,128)(2,1)S(1)} %collective-permute-done.30.from_x, bf16[128,1536]{1,0:T(8,128)(2,1)S(1)} %collective-permute-done.31.from_xz), custom_call_target="tpu_custom_call" | custom-call | bytes 3145728 | tf_op jit(solution)/shard_map/cond/branch_2_fun/unpack/pallas_call | solution.py:206
  90.9 1.7 %collective-permute-done.32.incoming = bf16[272,512]{1,0:T(8,128)(2,1)S(1)} collective-permute-done((bf16[272,512]{1,0:T(8,128)(2,1)S(1)}, bf16[272,512]{1,0:T(8,128)(2,1)S(1)}, u32[]{:S(2)}, u32[]{:S(2)}) %collective-permute-start.32) | collective-permute-done | bytes 278560 | tf_op jit(solution)/shard_map/cond/branch_2_fun/ppermute | solution.py:53
  92.6 0.8 combine.6
  (16 shorter events, 0.1 us)
Async XLA Ops:
  1.3 0.7 copy-start.20
  2.6 14.5 %copy-start.18 = (bf16[1,128,512]{2,1,0:T(8,128)(2,1)S(1)}, bf16[1,128,512]{2,1,0:T(8,128)(2,1)}, u32[]{:S(2)}) copy-start(bf16[1,128,512]{2,1,0:T(8,128)(2,1)} %get-tuple-element.129) | copy-start | bytes 393220 | tf_op jit(solution)/shard_map/cond
  3.6 25.9 %collective-permute-start.23 = (bf16[256,512]{1,0:T(8,128)(2,1)S(1)}, bf16[256,512]{1,0:T(8,128)(2,1)S(1)}, u32[]{:S(2)}, u32[]{:S(2)}) collective-permute-start(bf16[256,512]{1,0:T(8,128)(2,1)S(1)} %divide_convert_fusion.2.w0), channel_id=1, source_target_pairs={{0,2},{2,4},{4,6},{6,0},{1,3},{3,5},{5,7},{7,1},{8,10},{10,12},{12... | collective-permute-start | bytes 786440 | tf_op jit(solution)/shard_map/cond/branch_2_fun/ppermute | solution.py:40
  10.3 21.3 %collective-permute-start.22 = (bf16[256,512]{1,0:T(8,128)(2,1)S(1)}, bf16[256,512]{1,0:T(8,128)(2,1)S(1)}, u32[]{:S(2)}, u32[]{:S(2)}) collective-permute-start(bf16[256,512]{1,0:T(8,128)(2,1)S(1)} %divide_convert_fusion.2.w0), channel_id=1, source_target_pairs={{0,6},{2,0},{4,2},{6,4},{1,7},{3,1},{5,3},{7,5},{8,14},{10,8},{12,... | collective-permute-start | bytes 786440 | tf_op jit(solution)/shard_map/cond/branch_2_fun/ppermute | solution.py:40
  18.5 26.8 %collective-permute-start.26 = (bf16[128,1536]{1,0:T(8,128)(2,1)S(1)}, bf16[128,1536]{1,0:T(8,128)(2,1)S(1)}, u32[]{:S(2)}, u32[]{:S(2)}) collective-permute-start(bf16[128,1536]{1,0:T(8,128)(2,1)S(1)} %get-tuple-element.131), channel_id=1, source_target_pairs={{0,1},{1,0},{2,3},{3,2},{4,5},{5,4},{6,7},{7,6},{8,9},{9,8},{10,11... | collective-permute-start | bytes 1179656 | tf_op jit(solution)/shard_map/cond/branch_2_fun/ppermute | solution.py:48
  22.7 22.6 %collective-permute-start.27 = (bf16[128,1536]{1,0:T(8,128)(2,1)S(1)}, bf16[128,1536]{1,0:T(8,128)(2,1)S(1)}, u32[]{:S(2)}, u32[]{:S(2)}) collective-permute-start(bf16[128,1536]{1,0:T(8,128)(2,1)S(1)} %get-tuple-element.132), channel_id=1, source_target_pairs={{0,8},{1,9},{2,10},{3,11},{4,12},{5,13},{6,14},{7,15},{8,0},{9,1},... | collective-permute-start | bytes 1179656 | tf_op jit(solution)/shard_map/cond/branch_2_fun/ppermute | solution.py:48
  27.4 17.9 %collective-permute-start.28 = (bf16[128,1536]{1,0:T(8,128)(2,1)S(1)}, bf16[128,1536]{1,0:T(8,128)(2,1)S(1)}, u32[]{:S(2)}, u32[]{:S(2)}) collective-permute-start(bf16[128,1536]{1,0:T(8,128)(2,1)S(1)} %get-tuple-element.133), channel_id=1, source_target_pairs={{0,9},{1,8},{2,11},{3,10},{4,13},{5,12},{6,15},{7,14},{8,1},{9,0},... | collective-permute-start | bytes 1179656 | tf_op jit(solution)/shard_map/cond/branch_2_fun/ppermute | solution.py:48
  29.6 2.0 %copy-start.4 = (bf16[256,512]{1,0:T(8,128)(2,1)}, bf16[256,512]{1,0:T(8,128)(2,1)S(1)}, u32[]{:S(2)}) copy-start(bf16[256,512]{1,0:T(8,128)(2,1)S(1)} %collective-permute-done.23.w3) | copy-start | bytes 786436 | tf_op jit(solution)/shard_map/cond
  29.6 9.9 %collective-permute-start.24 = (bf16[128,512]{1,0:T(8,128)(2,1)S(1)}, bf16[128,512]{1,0:T(8,128)(2,1)S(1)}, u32[]{:S(2)}, u32[]{:S(2)}) collective-permute-start(bf16[128,512]{1,0:T(8,128)(2,1)S(1)} %slice.28), channel_id=1, source_target_pairs={{0,2},{2,4},{4,6},{6,0},{1,3},{3,5},{5,7},{7,1},{8,10},{10,12},{12... | collective-permute-start | bytes 393224 | tf_op jit(solution)/shard_map/cond/branch_2_fun/ppermute | solution.py:40
  31.6 13.7 %copy-start.12 = (bf16[256,512]{1,0:T(8,128)(2,1)}, bf16[256,512]{1,0:T(8,128)(2,1)S(1)}, u32[]{:S(2)}) copy-start(bf16[256,512]{1,0:T(8,128)(2,1)S(1)} %collective-permute-done.22.w1) | copy-start | bytes 786436 | tf_op jit(solution)/shard_map/cond
  31.6 13.7 %collective-permute-start.25 = (bf16[128,512]{1,0:T(8,128)(2,1)S(1)}, bf16[128,512]{1,0:T(8,128)(2,1)S(1)}, u32[]{:S(2)}, u32[]{:S(2)}) collective-permute-start(bf16[128,512]{1,0:T(8,128)(2,1)S(1)} %slice.29), channel_id=1, source_target_pairs={{0,6},{2,0},{4,2},{6,4},{1,7},{3,1},{5,3},{7,5},{8,14},{10,8},{12,... | collective-permute-start | bytes 393224 | tf_op jit(solution)/shard_map/cond/branch_2_fun/ppermute | solution.py:40
  48.3 30.3 %all-to-all-start.2 = ((bf16[4,256,512]{2,1,0:T(8,128)(2,1)}), bf16[4,256,512]{2,1,0:T(8,128)(2,1)S(1)}, u32[]{:S(2)}, u32[]{:S(2)}) async-start(bf16[4,256,512]{2,1,0:T(8,128)(2,1)} %share.6), calls=%async_computation.2 | async-start | bytes 2097152 | tf_op jit(solution)/shard_map/cond/branch_2_fun/all_to_all | solution.py:44
  53.3 1.0 %copy-start.5 = (bf16[256,512]{1,0:T(8,128)(2,1)S(1)}, bf16[256,512]{1,0:T(8,128)(2,1)}, u32[]{:S(2)}) copy-start(bf16[256,512]{1,0:T(8,128)(2,1)} %copy-done.4) | copy-start | bytes 786436 | tf_op jit(solution)/shard_map/cond
  54.2 0.9 %copy-start.13 = (bf16[256,512]{1,0:T(8,128)(2,1)S(1)}, bf16[256,512]{1,0:T(8,128)(2,1)}, u32[]{:S(2)}) copy-start(bf16[256,512]{1,0:T(8,128)(2,1)} %copy-done.12) | copy-start | bytes 786436 | tf_op jit(solution)/shard_map/cond
  57.5 26.8 %collective-permute-start.29 = (bf16[128,1536]{1,0:T(8,128)(2,1)}, bf16[128,1536]{1,0:T(8,128)(2,1)S(1)}, u32[]{:S(2)}, u32[]{:S(2)}) collective-permute-start(bf16[128,1536]{1,0:T(8,128)(2,1)} %get-tuple-element.143), channel_id=1, source_target_pairs={{0,1},{1,0},{2,3},{3,2},{4,5},{5,4},{6,7},{7,6},{8,9},{9,8},{10,11... | collective-permute-start | bytes 1179656 | tf_op jit(solution)/shard_map/cond/branch_2_fun/ppermute | solution.py:48
  61.8 22.4 %collective-permute-start.30 = (bf16[128,1536]{1,0:T(8,128)(2,1)}, bf16[128,1536]{1,0:T(8,128)(2,1)S(1)}, u32[]{:S(2)}, u32[]{:S(2)}) collective-permute-start(bf16[128,1536]{1,0:T(8,128)(2,1)} %get-tuple-element.144), channel_id=1, source_target_pairs={{0,8},{1,9},{2,10},{3,11},{4,12},{5,13},{6,14},{7,15},{8,0},{9,1},... | collective-permute-start | bytes 1179656 | tf_op jit(solution)/shard_map/cond/branch_2_fun/ppermute | solution.py:48
  64.7 25.0 %collective-permute-start.31 = (bf16[128,1536]{1,0:T(8,128)(2,1)}, bf16[128,1536]{1,0:T(8,128)(2,1)S(1)}, u32[]{:S(2)}, u32[]{:S(2)}) collective-permute-start(bf16[128,1536]{1,0:T(8,128)(2,1)} %get-tuple-element.145), channel_id=1, source_target_pairs={{0,9},{1,8},{2,11},{3,10},{4,13},{5,12},{6,15},{7,14},{8,1},{9,0},... | collective-permute-start | bytes 1179656 | tf_op jit(solution)/shard_map/cond/branch_2_fun/ppermute | solution.py:48
  81.0 11.6 %collective-permute-start.32 = (bf16[272,512]{1,0:T(8,128)(2,1)S(1)}, bf16[272,512]{1,0:T(8,128)(2,1)S(1)}, u32[]{:S(2)}, u32[]{:S(2)}) collective-permute-start(bf16[272,512]{1,0:T(8,128)(2,1)S(1)} %get-tuple-element.152.sent), channel_id=1, source_target_pairs={{0,64},{16,80},{32,96},{48,112},{64,128},{80,144},{96,160},{112,17... | collective-permute-start | bytes 835592 | tf_op jit(solution)/shard_map/cond/branch_2_fun/ppermute | solution.py:53

commit v4 on v3

--- a/solution.py
+++ b/solution.py
@@ -58,7 +58,7 @@
 SMEM = pl.BlockSpec(memory_space=pltpu.SMEM)
 
 
-def params_of(flops=0, moved=0, mib=48):
+def params_of(flops=0, moved=0, mib=24):
     return dict(
         compiler_params=pltpu.CompilerParams(vmem_limit_bytes=mib << 20),
         cost_estimate=pl.CostEstimate(flops=flops, bytes_accessed=moved, transcendentals=0),
@@ -86,30 +86,37 @@
     )(tokens, cot)
 
 
-def share_kernel(t0, t1, t2, t3, c0, c1, c2, c3, out):
-    total = None
-    for tok, cot in ((t0, c0), (t1, c1), (t2, c2), (t3, c3)):
-        term = lax.dot_general(
-            tok[...], cot[...], (((0,), (0,)), ((), ())), preferred_element_type=F32
-        )
-        total = term if total is None else total + term
-    out[0] = total.astype(BF16)
+def share_kernel(b0, b1, b2, b3, out, total, sems):
+    copies = []
+    for q in range(4):
+        columns = slice(q * 256, (q + 1) * 256)
+        part = None
+        for block in (b0, b1, b2, b3):
+            term = lax.dot_general(
+                block[:, columns], block[:, 1024:], (((0,), (0,)), ((), ())), preferred_element_type=F32
+            )
+            part = term if part is None else part + term
+        total[q] = part.astype(BF16)
+        copy = pltpu.make_async_copy(total.at[q], out.at[q], sems.at[q])
+        copy.start()
+        copies.append(copy)
+    for copy in copies:
+        copy.wait()
 
 
 def share(blocks):
     return pl.pallas_call(
         share_kernel,
-        grid=(4,),
-        in_specs=[pl.BlockSpec((128, 256), lambda q: (0, q))] * 4
-        + [pl.BlockSpec((128, 512), lambda q: (0, 2))] * 4,
-        out_specs=pl.BlockSpec((1, 256, 512), lambda q: (q, 0, 0)),
+        in_specs=[VMEM] * 4,
+        out_specs=ANY,
         out_shape=pltpu.HBM((4, 256, 512), BF16),
+        scratch_shapes=[pltpu.VMEM((4, 256, 512), BF16), pltpu.SemaphoreType.DMA((4,))],
         name="share",
-        **params_of(0, SHARE),
-    )(*blocks, *blocks)
-
-
-def product_kernel(b0, b1, b2, b3, w0, w1, w2, w3, own, to_z, to_x, to_xz, got):
+        **params_of(2 * 512 * 1024 * 512, 3 << 20),
+    )(*blocks)
+
+
+def product_kernel(weight, b0, b1, b2, b3, w0, w1, w2, w3, own, to_z, to_x, to_xz, got):
     quad = lax.axis_index("zq")
     for k, block in enumerate((b0, b1, b2, b3)):
         got[k * 128 : (k + 1) * 128, :] = block[...]
@@ -118,10 +125,11 @@
     keys = None
     for q, w in enumerate((w0, w1, w2, w3)):
         columns = pl.ds(pl.multiple_of(lax.rem(quad + q, 4) * 256, 256), 256)
-        term = jnp.dot(got[:, columns], w[...], preferred_element_type=F32)
+        w = (w[...].astype(F32) / weight[0]).astype(BF16)
+        term = jnp.dot(got[:, columns], w, preferred_element_type=F32)
         keys = term if keys is None else keys + term
         part = lax.dot_general(
-            cot, w[...], (((1,), (1,)), ((), ())), preferred_element_type=F32
+            cot, w, (((1,), (1,)), ((), ())), preferred_element_type=F32
         ).astype(BF16)
         for k, out in enumerate(outs):
             out[:, columns] = part[k * 128 : (k + 1) * 128, :]
@@ -130,43 +138,79 @@
         out[:, 1024:] = keys[k * 128 : (k + 1) * 128, :]
 
 
-def products(blocks, w):
+def products(weight, blocks, w):
     block = jax.ShapeDtypeStruct((128, 1536), BF16)
     return pl.pallas_call(
         product_kernel,
-        in_specs=[VMEM] * 8,
+        in_specs=[SMEM] + [VMEM] * 8,
         out_specs=[VMEM] * 4,
         out_shape=[block] * 4,
         scratch_shapes=[pltpu.VMEM((512, 1536), BF16)],
         name="products",
         **params_of(4 * 512 * 1024 * 512, 4 << 20),
-    )(*blocks, *w)
-
-
-def adam_kernel(weight, bias, shares, first, second, numer, new_first, new_second, sent):
+    )(weight, *blocks, *w)
+
+
+def stage_kernel(first, second, numer, first_out, second_out, numer_out):
+    first_out[...] = first[...]
+    second_out[...] = second[...]
+    numer_out[...] = numer[...]
+
+
+def stage(first, second, numer):
+    state = jax.ShapeDtypeStruct((256, 512), F32)
+    return pl.pallas_call(
+        stage_kernel,
+        in_specs=[VMEM] * 3,
+        out_specs=[VMEM] * 3,
+        out_shape=[state, state, jax.ShapeDtypeStruct((256, 512), BF16)],
+        name="stage",
+        **params_of(0, 2 << 20),
+    )(first, second, numer)
+
+
+def moments(shares, first, second):
     total = shares[0].astype(F32)
     for q in range(1, 4):
         total = total + shares[q].astype(F32)
     grad = total / 2048.0
     one = BETA_ONE * first[...] + (1.0 - BETA_ONE) * grad
     two = BETA_TWO * second[...] + (1.0 - BETA_TWO) * grad * grad
-    new_first[...] = one
-    new_second[...] = two
+    return one, two
+
+
+def adam_kernel(weight, bias, shares, first, second, numer, sent):
+    one, two = moments(shares, first, second)
     update = LEARN * (one / bias[0]) / (jnp.sqrt(two / bias[1]) + EPSILON)
     sent[:256, :] = (numer[...].astype(F32) - update).astype(BF16)
     sent[256:, :] = jnp.full((16, 512), weight[0], F32).astype(BF16)
 
 
 def adam(weight, bias, shares, first, second, numer):
-    state = jax.ShapeDtypeStruct((256, 512), F32)
     return pl.pallas_call(
         adam_kernel,
         in_specs=[SMEM, SMEM] + [VMEM] * 4,
-        out_specs=[VMEM] * 3,
-        out_shape=[state, state, jax.ShapeDtypeStruct((272, 512), BF16)],
+        out_specs=VMEM,
+        out_shape=jax.ShapeDtypeStruct((272, 512), BF16),
         name="adam",
-        **params_of(0, ADAM),
+        **params_of(0, 3 << 20),
     )(weight, bias, shares, first, second, numer)
+
+
+def state_kernel(shares, first, second, new_first, new_second):
+    new_first[...], new_second[...] = moments(shares, first, second)
+
+
+def new_state(shares, first, second):
+    state = jax.ShapeDtypeStruct((256, 512), F32)
+    return pl.pallas_call(
+        state_kernel,
+        in_specs=[VMEM] * 3,
+        out_specs=[VMEM] * 2,
+        out_shape=[state, state],
+        name="new_state",
+        **params_of(0, 3 << 20),
+    )(shares, first, second)
 
 
 def combine_kernel(sent, incoming, new_params, mixed):
@@ -219,24 +263,27 @@
     count = (tstep + 1).astype(F32)
     bias = 1.0 - jnp.power(jnp.array([BETA_ONE, BETA_TWO], F32), count)
 
-    debiased = (params[0].astype(F32) / mass[0]).astype(BF16)
-    w_down = along_quad(debiased, 1)
-    w_up = along_quad(debiased, -1)
+    numer = params[0]
+    w_down = along_quad(numer, 1)
+    w_up = along_quad(numer, -1)
     far = jnp.concatenate([along_quad(w_down[:128], 1), along_quad(w_up[128:], -1)], axis=0)
-    rows = [debiased, w_up, far, w_down]
+    rows = [numer, w_up, far, w_down]
     own, *sends = pack(tokens[0], cotangent[0])
-    blocks = [own] + [swap_features(x, r + 1) for r, x in enumerate(sends)]
-    rows, blocks = lax.optimization_barrier((rows, blocks))
-    shares = swap_tokens(share(blocks))
-
-    own, *sends = products(blocks, rows)
-    back = [swap_features(x, r + 1) for r, x in enumerate(sends)]
-
-    new_first, new_second, sent = adam(
-        mass, bias, shares, first_moment[0], second_moment[0], params[0]
-    )
+    far_first = [swap_features(sends[r], r + 1) for r in (2, 1, 0)]
+    blocks = [own] + far_first[::-1]
+    mine, rows = lax.optimization_barrier((share(blocks), rows))
+    shares = swap_tokens(mine)
+
+    own, *sends = products(mass, blocks, rows)
+    back = [swap_features(sends[r], r + 1) for r in (2, 1, 0)][::-1]
+
+    first, second, base = stage(first_moment[0], second_moment[0], params[0])
+    sent = adam(mass, bias, shares, first, second, base)
     incoming = pushed(sent, hop)
+    shares, sent = lax.optimization_barrier((shares, sent))
+    new_first, new_second = new_state(shares, first, second)
     new_params, mixed = combine(sent, incoming)
+    own, new_first = lax.optimization_barrier((own, new_first))
     token_grad, keys = unpack(own, *back)
     return (
         keys[None],

time: 94.5 us -> 92.8 us (0.982); the launches traced: 93.8 us -> 91 us
  waiting for transfers between devices: 25.4 us -> 21.5 us
  Pallas kernels: 11 us -> 12.3 us
    pallas_call x2 -> x4, Pallas kernels: 5.22 us -> 7.9 us  [the longest x1 3.29 us: products(): pl.pallas_call(product_kernel, in_specs=[SMEM] + [VMEM] * 8, out_specs=[V...]
    all_to_all x1, waiting for transfers between devices: 9.98 us -> 7.47 us  [swap_tokens(): return lax.all_to_all(x, 'zq', 0, 0, tiled=True)]
    ppermute x1, waiting for transfers between devices: 1.71 us -> 0.27 us  [pushed(): return lax.ppermute(outgoing, REPS, pairs)]
    pallas_call x1, Pallas kernels: 2.45 us -> 1.07 us  [adam(): pl.pallas_call(adam_kernel, in_specs=[SMEM, SMEM] + [VMEM] * 4, out_specs...]
    convert_element_type x1 -> x0, other arithmetic: 1.03 us -> none  [step_with(): debiased = (params[0].astype(F32) / mass[0]).astype(BF16)]
    cond x10 -> x18, local copies, waits for them, and re-layouts: 1.91 us -> 1.65 us
  transfers between devices with their start and end apart: 12 -> 12, of which waited for: 5 -> 5; matrix products, arithmetic and copies ran while one was open for 0% -> 1% of each run, Pallas kernels for 8% -> 10%
where the time goes in v4:
time: 92.8 us; the launch traced here: 91 us
  starting transfers between devices  50.8 us (55%)
  waiting for transfers between devices  21.5 us (23%)
  Pallas kernels  12.3 us (13%)
  local copies, waits for them, and re-layouts  2.32 us (2%)
  loops' own time  1.8 us (2%)
  between operations  1.47 us (2%)
    ppermute x6, starting transfers between devices, swap_features(): return lax.ppermute(x, PAIRS, partner_pairs(relative))  22.2 us
    ppermute x4, starting transfers between devices, along_quad(): return lax.ppermute(x, 'zq', [(i, (i + step) % 4) for i in range(4)])  20.8 us
    ppermute x4, waiting for transfers between devices, along_quad(): return lax.ppermute(x, 'zq', [(i, (i + step) % 4) for i in range(4)])  8.3 us
    all_to_all x1, waiting for transfers between devices, swap_tokens(): return lax.all_to_all(x, 'zq', 0, 0, tiled=True)  7.47 us
    ppermute x6, waiting for transfers between devices, swap_features(): return lax.ppermute(x, PAIRS, partner_pairs(relative))  5.51 us
    all_to_all x1, starting transfers between devices, swap_tokens(): return lax.all_to_all(x, 'zq', 0, 0, tiled=True)  4.33 us
    ppermute x1, starting transfers between devices, pushed(): return lax.ppermute(outgoing, REPS, pairs)  3.52 us
    pallas_call x1, Pallas kernels, products(): pl.pallas_call(product_kernel, in_specs=[SMEM] + [VMEM] * 8, out_specs=[V...  3.29 us
  transfers between devices with their start and end apart: 12, of which 5 were waited for; matrix products, arithmetic and copies ran while one was open for 1% of the time, Pallas kernels for 10%

profile of v4, /device:TPU:1, one launch (start us, length us, event | category | flops | bytes accessed | tf_op | source)
XLA Modules:
  0.0 91.0 jit_solution(17107604420715297800)
XLA Ops:
  1.3 0.6 copy-done.36
  1.9 88.9 %conditional.1 = (f32[1]{0:T(128)}, bf16[1,128,512]{2,1,0:T(8,128)(2,1)}, bf16[1,128,4096]{2,1,0:T(8,128)(2,1)}, bf16[1,256,512]{2,1,0:T(8,128)(2,1)}, f32[1,256,512]{2,1,0:T(8,128)}, /*index=5*/f32[1,256,512]{2,1,0:T(8,128)}) conditional(s32[]{:T(128)} %bitcast.44, (bf16[1]{0:T(256)(128)(2,1)}, ...), branch_computations={%region_0.0_spmd, %region_1.0_spmd, %region_2.0_spmd, %region_3.0_... | conditional | flops 1611137024 | bytes 118555456 | solution.py:300
  1.9 6.6 %collective-permute-start.4 = (bf16[256,512]{1,0:T(8,128)(2,1)}, bf16[256,512]{1,0:T(8,128)(2,1)S(1)}, u32[]{:S(2)}, u32[]{:S(2)}) collective-permute-start(bf16[256,512]{1,0:T(8,128)(2,1)} %bitcast.57), channel_id=1, source_target_pairs={{0,2},{2,4},{4,6},{6,0},{1,3},{3,5},{5,7},{7,1},{8,10},{10,12},{12... | collective-permute-start | bytes 786440 | tf_op jit(solution)/shard_map/cond/branch_0_fun/ppermute | solution.py:40
  8.6 6.8 %collective-permute-start.3 = (bf16[256,512]{1,0:T(8,128)(2,1)}, bf16[256,512]{1,0:T(8,128)(2,1)S(1)}, u32[]{:S(2)}, u32[]{:S(2)}) collective-permute-start(bf16[256,512]{1,0:T(8,128)(2,1)} %bitcast.58), channel_id=1, source_target_pairs={{0,6},{2,0},{4,2},{6,4},{1,7},{3,1},{5,3},{7,5},{8,14},{10,8},{12,... | collective-permute-start | bytes 786440 | tf_op jit(solution)/shard_map/cond/branch_0_fun/ppermute | solution.py:40
  15.4 1.4 %pack.4 = (bf16[128,1536]{1,0:T(8,128)(2,1)S(1)}, bf16[128,1536]{1,0:T(8,128)(2,1)S(1)}, bf16[128,1536]{1,0:T(8,128)(2,1)S(1)}, bf16[128,1536]{1,0:T(8,128)(2,1)S(1)}) custom-call(bf16[128,4096]{1,0:T(8,128)(2,1)} %bitcast.45, bf16[128,512]{1,0:T(8,128)(2,1)} %bitcast.73), custom_call_target="tpu_custom_call" | custom-call | bytes 3145728 | tf_op jit(solution)/shard_map/cond/branch_0_fun/pack/pallas_call | solution.py:79
  16.7 4.3 %collective-permute-start = (bf16[128,1536]{1,0:T(8,128)(2,1)S(1)}, bf16[128,1536]{1,0:T(8,128)(2,1)S(1)}, u32[]{:S(2)}, u32[]{:S(2)}) collective-permute-start(bf16[128,1536]{1,0:T(8,128)(2,1)S(1)} %get-tuple-element.68), channel_id=1, source_target_pairs={{0,1},{1,0},{2,3},{3,2},{4,5},{5,4},{6,7},{7,6},{8,9},{9,8},{10,11... | collective-permute-start | bytes 1179656 | tf_op jit(solution)/shard_map/cond/branch_0_fun/ppermute | solution.py:48
  21.0 4.7 %collective-permute-start.1 = (bf16[128,1536]{1,0:T(8,128)(2,1)S(1)}, bf16[128,1536]{1,0:T(8,128)(2,1)S(1)}, u32[]{:S(2)}, u32[]{:S(2)}) collective-permute-start(bf16[128,1536]{1,0:T(8,128)(2,1)S(1)} %get-tuple-element.69), channel_id=1, source_target_pairs={{0,8},{1,9},{2,10},{3,11},{4,12},{5,13},{6,14},{7,15},{8,0},{9,1},... | collective-permute-start | bytes 1179656 | tf_op jit(solution)/shard_map/cond/branch_0_fun/ppermute | solution.py:48
  25.7 2.2 %collective-permute-start.2 = (bf16[128,1536]{1,0:T(8,128)(2,1)S(1)}, bf16[128,1536]{1,0:T(8,128)(2,1)S(1)}, u32[]{:S(2)}, u32[]{:S(2)}) collective-permute-start(bf16[128,1536]{1,0:T(8,128)(2,1)S(1)} %get-tuple-element.70), channel_id=1, source_target_pairs={{0,9},{1,8},{2,11},{3,10},{4,13},{5,12},{6,15},{7,14},{8,1},{9,0},... | collective-permute-start | bytes 1179656 | tf_op jit(solution)/shard_map/cond/branch_0_fun/ppermute | solution.py:48
  27.9 1.9 %collective-permute-start.5 = (bf16[128,512]{1,0:T(8,128)(2,1)S(1)}, bf16[128,512]{1,0:T(8,128)(2,1)S(1)}, u32[]{:S(2)}, u32[]{:S(2)}) collective-permute-start(bf16[128,512]{1,0:T(8,128)(2,1)S(1)} %slice.24), channel_id=1, source_target_pairs={{0,2},{2,4},{4,6},{6,0},{1,3},{3,5},{5,7},{7,1},{8,10},{10,12},{12... | collective-permute-start | bytes 393224 | tf_op jit(solution)/shard_map/cond/branch_0_fun/ppermute | solution.py:40
  29.9 5.5 %collective-permute-start.6 = (bf16[128,512]{1,0:T(8,128)(2,1)S(1)}, bf16[128,512]{1,0:T(8,128)(2,1)S(1)}, u32[]{:S(2)}, u32[]{:S(2)}) collective-permute-start(bf16[128,512]{1,0:T(8,128)(2,1)S(1)} %slice.25), channel_id=1, source_target_pairs={{0,6},{2,0},{4,2},{6,4},{1,7},{3,1},{5,3},{7,5},{8,14},{10,8},{12,... | collective-permute-start | bytes 393224 | tf_op jit(solution)/shard_map/cond/branch_0_fun/ppermute | solution.py:40
  35.3 2.5 %collective-permute-done.5 = bf16[128,512]{1,0:T(8,128)(2,1)S(1)} collective-permute-done((bf16[128,512]{1,0:T(8,128)(2,1)S(1)}, bf16[128,512]{1,0:T(8,128)(2,1)S(1)}, u32[]{:S(2)}, u32[]{:S(2)}) %collective-permute-start.5) | collective-permute-done | bytes 131104 | tf_op jit(solution)/shard_map/cond/branch_0_fun/ppermute | solution.py:40
  37.8 5.8 %collective-permute-done.6 = bf16[128,512]{1,0:T(8,128)(2,1)S(1)} collective-permute-done((bf16[128,512]{1,0:T(8,128)(2,1)S(1)}, bf16[128,512]{1,0:T(8,128)(2,1)S(1)}, u32[]{:S(2)}, u32[]{:S(2)}) %collective-permute-start.6) | collective-permute-done | bytes 131104 | tf_op jit(solution)/shard_map/cond/branch_0_fun/ppermute | solution.py:40
  43.6 0.7 pad_maximum_fusion.w2
  44.4 2.0 %share.4 = bf16[4,256,512]{2,1,0:T(8,128)(2,1)} custom-call(bf16[128,1536]{1,0:T(8,128)(2,1)S(1)} %get-tuple-element.67.b0, bf16[128,1536]{1,0:T(8,128)(2,1)S(1)} %collective-permute-done.b1, bf16[128,1536]{1,0:T(8,128)(2,1)S(1)} %collective-permute-done.1.b2, bf16[128,1536]{1,0:T(8,128)(2,1)S(1)} %collective-permute-done.2.b3), custom_call_target="tpu_custom_call" | custom-call | flops 536870912 | bytes 3145728 | tf_op jit(solution)/shard_map/cond/branch_0_fun/share/pallas_call | solution.py:108
  46.4 0.7 copy-done
  47.2 4.3 %all-to-all-start = ((bf16[4,256,512]{2,1,0:T(8,128)(2,1)}), bf16[4,256,512]{2,1,0:T(8,128)(2,1)S(1)}, u32[]{:S(2)}, u32[]{:S(2)}) async-start(bf16[4,256,512]{2,1,0:T(8,128)(2,1)} %share.4), calls=%async_computation | async-start | bytes 2097152 | tf_op jit(solution)/shard_map/cond/branch_0_fun/all_to_all | solution.py:44
  52.8 1.4 %stage.4 = (f32[256,512]{1,0:T(8,128)S(1)}, f32[256,512]{1,0:T(8,128)S(1)}, bf16[256,512]{1,0:T(8,128)(2,1)S(1)}) custom-call(f32[256,512]{1,0:T(8,128)} %bitcast.49, f32[256,512]{1,0:T(8,128)} %bitcast.53, bf16[256,512]{1,0:T(8,128)(2,1)} %bitcast.59), custom_call_target="tpu_custom_call" | custom-call | bytes 2097152 | tf_op jit(solution)/shard_map/cond/branch_0_fun/stage/pallas_call | solution.py:162
  54.3 0.0 copy-done.21
  54.3 0.1 copy-done.29
  54.4 3.3 %products.4 = (bf16[128,1536]{1,0:T(8,128)(2,1)S(1)}, bf16[128,1536]{1,0:T(8,128)(2,1)}, bf16[128,1536]{1,0:T(8,128)(2,1)}, bf16[128,1536]{1,0:T(8,128)(2,1)}) custom-call(f32[1]{0:T(128)S(6)} %convert_element_type.24.weight, bf16[128,1536]{1,0:T(8,128)(2,1)S(1)} %get-tuple-element.67.b0, bf16[128,1536]{1,0:T(8,128)(2,1)S(1)} %collective-permute-done.b1, ...), custom_call_target="tpu_custom_call" | custom-call | flops 1073741824 | bytes 4194304 | tf_op jit(solution)/shard_map/cond/branch_0_fun/products/pallas_call | solution.py:143
  57.7 0.8 copy-done.8
  58.5 4.0 %collective-permute-start.7 = (bf16[128,1536]{1,0:T(8,128)(2,1)}, bf16[128,1536]{1,0:T(8,128)(2,1)S(1)}, u32[]{:S(2)}, u32[]{:S(2)}) collective-permute-start(bf16[128,1536]{1,0:T(8,128)(2,1)} %get-tuple-element.88), channel_id=1, source_target_pairs={{0,1},{1,0},{2,3},{3,2},{4,5},{5,4},{6,7},{7,6},{8,9},{9,8},{10,11... | collective-permute-start | bytes 1179656 | tf_op jit(solution)/shard_map/cond/branch_0_fun/ppermute | solution.py:48
  62.4 2.9 %collective-permute-start.8 = (bf16[128,1536]{1,0:T(8,128)(2,1)}, bf16[128,1536]{1,0:T(8,128)(2,1)S(1)}, u32[]{:S(2)}, u32[]{:S(2)}) collective-permute-start(bf16[128,1536]{1,0:T(8,128)(2,1)} %get-tuple-element.89), channel_id=1, source_target_pairs={{0,8},{1,9},{2,10},{3,11},{4,12},{5,13},{6,14},{7,15},{8,0},{9,1},... | collective-permute-start | bytes 1179656 | tf_op jit(solution)/shard_map/cond/branch_0_fun/ppermute | solution.py:48
  65.4 4.2 %collective-permute-start.9 = (bf16[128,1536]{1,0:T(8,128)(2,1)}, bf16[128,1536]{1,0:T(8,128)(2,1)S(1)}, u32[]{:S(2)}, u32[]{:S(2)}) collective-permute-start(bf16[128,1536]{1,0:T(8,128)(2,1)} %get-tuple-element.90), channel_id=1, source_target_pairs={{0,9},{1,8},{2,11},{3,10},{4,13},{5,12},{6,15},{7,14},{8,1},{9,0},... | collective-permute-start | bytes 1179656 | tf_op jit(solution)/shard_map/cond/branch_0_fun/ppermute | solution.py:48
  69.6 7.5 %all-to-all-done.shares = bf16[4,256,512]{2,1,0:T(8,128)(2,1)S(1)} async-done(((bf16[4,256,512]{2,1,0:T(8,128)(2,1)}), bf16[4,256,512]{2,1,0:T(8,128)(2,1)S(1)}, u32[]{:S(2)}, u32[]{:S(2)}) %all-to-all-start) | async-done | bytes 1048608 | tf_op jit(solution)/shard_map/cond/branch_0_fun/all_to_all | solution.py:44
  77.1 1.1 %adam.4.sent = bf16[272,512]{1,0:T(8,128)(2,1)S(1)} custom-call(f32[1]{0:T(128)S(6)} %convert_element_type.24.weight, f32[2]{0:T(128)S(1)} %power_subtract_fusion.bias, bf16[4,256,512]{2,1,0:T(8,128)(2,1)S(1)} %all-to-all-done.shares, f32[256,512]{1,0:T(8,128)S(1)} %get-tuple-element.82.first, f32[256,512]{1,0:T(8,128)S(1)} %get-tuple-element.83.second, ...), custom_call_target="tpu_custom_call" | custom-call | bytes 3145728 | tf_op jit(solution)/shard_map/cond/branch_0_fun/adam/pallas_call | solution.py:190
  78.1 3.5 %collective-permute-start.10 = (bf16[272,512]{1,0:T(8,128)(2,1)S(1)}, bf16[272,512]{1,0:T(8,128)(2,1)S(1)}, u32[]{:S(2)}, u32[]{:S(2)}) collective-permute-start(bf16[272,512]{1,0:T(8,128)(2,1)S(1)} %adam.4.sent), channel_id=1, source_target_pairs={{0,16},{16,32},{32,48},{48,64},{64,80},{80,96},{96,112},{112,128},... | collective-permute-start | bytes 835592 | tf_op jit(solution)/shard_map/cond/branch_0_fun/ppermute | solution.py:53
  81.7 1.2 %new_state.4 = (f32[256,512]{1,0:T(8,128)}, f32[256,512]{1,0:T(8,128)}) custom-call(bf16[4,256,512]{2,1,0:T(8,128)(2,1)S(1)} %all-to-all-done.shares, f32[256,512]{1,0:T(8,128)S(1)} %get-tuple-element.82.first, f32[256,512]{1,0:T(8,128)S(1)} %get-tuple-element.83.second), custom_call_target="tpu_custom_call" | custom-call | bytes 3145728 | tf_op jit(solution)/shard_map/cond/branch_0_fun/new_state/pallas_call | solution.py:206
  82.8 5.5 %collective-permute-done.9.from_xz = bf16[128,1536]{1,0:T(8,128)(2,1)S(1)} collective-permute-done((bf16[128,1536]{1,0:T(8,128)(2,1)}, bf16[128,1536]{1,0:T(8,128)(2,1)S(1)}, u32[]{:S(2)}, u32[]{:S(2)}) %collective-permute-start.9) | collective-permute-done | bytes 393248 | tf_op jit(solution)/shard_map/cond/branch_0_fun/ppermute | solution.py:48
  88.3 1.1 %unpack.4 = (bf16[128,4096]{1,0:T(8,128)(2,1)}, bf16[128,512]{1,0:T(8,128)(2,1)}) custom-call(bf16[128,1536]{1,0:T(8,128)(2,1)S(1)} %copy-done.9, bf16[128,1536]{1,0:T(8,128)(2,1)S(1)} %collective-permute-done.7.from_z, bf16[128,1536]{1,0:T(8,128)(2,1)S(1)} %collective-permute-done.8.from_x, bf16[128,1536]{1,0:T(8,128)(2,1)S(1)} %collective-permute-done.9.from_xz), custom_call_target="tpu_custom_call" | custom-call | bytes 3145728 | tf_op jit(solution)/shard_map/cond/branch_0_fun/unpack/pallas_call | solution.py:250
  89.5 0.3 collective-permute-done.10.incoming
  89.7 0.8 combine.4
  (25 shorter events, 0.1 us)
Async XLA Ops:
  1.3 0.7 copy-start.36
  1.9 25.9 %collective-permute-start.4 = (bf16[256,512]{1,0:T(8,128)(2,1)}, bf16[256,512]{1,0:T(8,128)(2,1)S(1)}, u32[]{:S(2)}, u32[]{:S(2)}) collective-permute-start(bf16[256,512]{1,0:T(8,128)(2,1)} %bitcast.57), channel_id=1, source_target_pairs={{0,2},{2,4},{4,6},{6,0},{1,3},{3,5},{5,7},{7,1},{8,10},{10,12},{12... | collective-permute-start | bytes 786440 | tf_op jit(solution)/shard_map/cond/branch_0_fun/ppermute | solution.py:40
  8.6 21.3 %collective-permute-start.3 = (bf16[256,512]{1,0:T(8,128)(2,1)}, bf16[256,512]{1,0:T(8,128)(2,1)S(1)}, u32[]{:S(2)}, u32[]{:S(2)}) collective-permute-start(bf16[256,512]{1,0:T(8,128)(2,1)} %bitcast.58), channel_id=1, source_target_pairs={{0,6},{2,0},{4,2},{6,4},{1,7},{3,1},{5,3},{7,5},{8,14},{10,8},{12,... | collective-permute-start | bytes 786440 | tf_op jit(solution)/shard_map/cond/branch_0_fun/ppermute | solution.py:40
  16.7 27.6 %collective-permute-start = (bf16[128,1536]{1,0:T(8,128)(2,1)S(1)}, bf16[128,1536]{1,0:T(8,128)(2,1)S(1)}, u32[]{:S(2)}, u32[]{:S(2)}) collective-permute-start(bf16[128,1536]{1,0:T(8,128)(2,1)S(1)} %get-tuple-element.68), channel_id=1, source_target_pairs={{0,1},{1,0},{2,3},{3,2},{4,5},{5,4},{6,7},{7,6},{8,9},{9,8},{10,11... | collective-permute-start | bytes 1179656 | tf_op jit(solution)/shard_map/cond/branch_0_fun/ppermute | solution.py:48
  21.0 23.4 %collective-permute-start.1 = (bf16[128,1536]{1,0:T(8,128)(2,1)S(1)}, bf16[128,1536]{1,0:T(8,128)(2,1)S(1)}, u32[]{:S(2)}, u32[]{:S(2)}) collective-permute-start(bf16[128,1536]{1,0:T(8,128)(2,1)S(1)} %get-tuple-element.69), channel_id=1, source_target_pairs={{0,8},{1,9},{2,10},{3,11},{4,12},{5,13},{6,14},{7,15},{8,0},{9,1},... | collective-permute-start | bytes 1179656 | tf_op jit(solution)/shard_map/cond/branch_0_fun/ppermute | solution.py:48
  25.7 18.7 %collective-permute-start.2 = (bf16[128,1536]{1,0:T(8,128)(2,1)S(1)}, bf16[128,1536]{1,0:T(8,128)(2,1)S(1)}, u32[]{:S(2)}, u32[]{:S(2)}) collective-permute-start(bf16[128,1536]{1,0:T(8,128)(2,1)S(1)} %get-tuple-element.70), channel_id=1, source_target_pairs={{0,9},{1,8},{2,11},{3,10},{4,13},{5,12},{6,15},{7,14},{8,1},{9,0},... | collective-permute-start | bytes 1179656 | tf_op jit(solution)/shard_map/cond/branch_0_fun/ppermute | solution.py:48
  27.9 16.5 %copy-start.20 = (bf16[256,512]{1,0:T(8,128)(2,1)}, bf16[256,512]{1,0:T(8,128)(2,1)S(1)}, u32[]{:S(2)}) copy-start(bf16[256,512]{1,0:T(8,128)(2,1)S(1)} %collective-permute-done.4.w3) | copy-start | bytes 786436 | tf_op jit(solution)/shard_map/cond
  27.9 9.9 %collective-permute-start.5 = (bf16[128,512]{1,0:T(8,128)(2,1)S(1)}, bf16[128,512]{1,0:T(8,128)(2,1)S(1)}, u32[]{:S(2)}, u32[]{:S(2)}) collective-permute-start(bf16[128,512]{1,0:T(8,128)(2,1)S(1)} %slice.24), channel_id=1, source_target_pairs={{0,2},{2,4},{4,6},{6,0},{1,3},{3,5},{5,7},{7,1},{8,10},{10,12},{12... | collective-permute-start | bytes 393224 | tf_op jit(solution)/shard_map/cond/branch_0_fun/ppermute | solution.py:40
  29.8 14.5 %copy-start.28 = (bf16[256,512]{1,0:T(8,128)(2,1)}, bf16[256,512]{1,0:T(8,128)(2,1)S(1)}, u32[]{:S(2)}) copy-start(bf16[256,512]{1,0:T(8,128)(2,1)S(1)} %collective-permute-done.3.w1) | copy-start | bytes 786436 | tf_op jit(solution)/shard_map/cond
  29.9 13.8 %collective-permute-start.6 = (bf16[128,512]{1,0:T(8,128)(2,1)S(1)}, bf16[128,512]{1,0:T(8,128)(2,1)S(1)}, u32[]{:S(2)}, u32[]{:S(2)}) collective-permute-start(bf16[128,512]{1,0:T(8,128)(2,1)S(1)} %slice.25), channel_id=1, source_target_pairs={{0,6},{2,0},{4,2},{6,4},{1,7},{3,1},{5,3},{7,5},{8,14},{10,8},{12,... | collective-permute-start | bytes 393224 | tf_op jit(solution)/shard_map/cond/branch_0_fun/ppermute | solution.py:40
  46.4 0.7 copy-start
  47.2 29.9 %all-to-all-start = ((bf16[4,256,512]{2,1,0:T(8,128)(2,1)}), bf16[4,256,512]{2,1,0:T(8,128)(2,1)S(1)}, u32[]{:S(2)}, u32[]{:S(2)}) async-start(bf16[4,256,512]{2,1,0:T(8,128)(2,1)} %share.4), calls=%async_computation | async-start | bytes 2097152 | tf_op jit(solution)/shard_map/cond/branch_0_fun/all_to_all | solution.py:44
  52.8 1.5 %copy-start.1 = (bf16[128,1536]{1,0:T(8,128)(2,1)S(1)}, bf16[128,1536]{1,0:T(8,128)(2,1)}, u32[]{:S(2)}) copy-start(bf16[128,1536]{1,0:T(8,128)(2,1)} %copy-done) | copy-start | bytes 1179652 | tf_op jit(solution)/shard_map/cond
  52.8 1.5 %copy-start.16 = (bf16[256,512]{1,0:T(8,128)(2,1)S(1)}, bf16[256,512]{1,0:T(8,128)(2,1)}, u32[]{:S(2)}) copy-start(bf16[256,512]{1,0:T(8,128)(2,1)} %pad_maximum_fusion.w2) | copy-start | bytes 786436 | tf_op jit(solution)/shard_map/cond
  52.8 1.5 %copy-start.21 = (bf16[256,512]{1,0:T(8,128)(2,1)S(1)}, bf16[256,512]{1,0:T(8,128)(2,1)}, u32[]{:S(2)}) copy-start(bf16[256,512]{1,0:T(8,128)(2,1)} %copy-done.20) | copy-start | bytes 786436 | tf_op jit(solution)/shard_map/cond
  52.8 1.6 %copy-start.29 = (bf16[256,512]{1,0:T(8,128)(2,1)S(1)}, bf16[256,512]{1,0:T(8,128)(2,1)}, u32[]{:S(2)}) copy-start(bf16[256,512]{1,0:T(8,128)(2,1)} %copy-done.28) | copy-start | bytes 786436 | tf_op jit(solution)/shard_map/cond
  57.7 0.8 copy-start.8
  58.5 24.4 %collective-permute-start.7 = (bf16[128,1536]{1,0:T(8,128)(2,1)}, bf16[128,1536]{1,0:T(8,128)(2,1)S(1)}, u32[]{:S(2)}, u32[]{:S(2)}) collective-permute-start(bf16[128,1536]{1,0:T(8,128)(2,1)} %get-tuple-element.88), channel_id=1, source_target_pairs={{0,1},{1,0},{2,3},{3,2},{4,5},{5,4},{6,7},{7,6},{8,9},{9,8},{10,11... | collective-permute-start | bytes 1179656 | tf_op jit(solution)/shard_map/cond/branch_0_fun/ppermute | solution.py:48
  62.4 20.4 %collective-permute-start.8 = (bf16[128,1536]{1,0:T(8,128)(2,1)}, bf16[128,1536]{1,0:T(8,128)(2,1)S(1)}, u32[]{:S(2)}, u32[]{:S(2)}) collective-permute-start(bf16[128,1536]{1,0:T(8,128)(2,1)} %get-tuple-element.89), channel_id=1, source_target_pairs={{0,8},{1,9},{2,10},{3,11},{4,12},{5,13},{6,14},{7,15},{8,0},{9,1},... | collective-permute-start | bytes 1179656 | tf_op jit(solution)/shard_map/cond/branch_0_fun/ppermute | solution.py:48
  65.4 22.9 %collective-permute-start.9 = (bf16[128,1536]{1,0:T(8,128)(2,1)}, bf16[128,1536]{1,0:T(8,128)(2,1)S(1)}, u32[]{:S(2)}, u32[]{:S(2)}) collective-permute-start(bf16[128,1536]{1,0:T(8,128)(2,1)} %get-tuple-element.90), channel_id=1, source_target_pairs={{0,9},{1,8},{2,11},{3,10},{4,13},{5,12},{6,15},{7,14},{8,1},{9,0},... | collective-permute-start | bytes 1179656 | tf_op jit(solution)/shard_map/cond/branch_0_fun/ppermute | solution.py:48
  78.1 10.2 %copy-start.9 = (bf16[128,1536]{1,0:T(8,128)(2,1)S(1)}, bf16[128,1536]{1,0:T(8,128)(2,1)}, u32[]{:S(2)}) copy-start(bf16[128,1536]{1,0:T(8,128)(2,1)} %copy-done.8) | copy-start | bytes 1179652 | tf_op jit(solution)/shard_map/cond
  78.1 11.6 %collective-permute-start.10 = (bf16[272,512]{1,0:T(8,128)(2,1)S(1)}, bf16[272,512]{1,0:T(8,128)(2,1)S(1)}, u32[]{:S(2)}, u32[]{:S(2)}) collective-permute-start(bf16[272,512]{1,0:T(8,128)(2,1)S(1)} %adam.4.sent), channel_id=1, source_target_pairs={{0,16},{16,32},{32,48},{48,64},{64,80},{80,96},{96,112},{112,128},... | collective-permute-start | bytes 835592 | tf_op jit(solution)/shard_map/cond/branch_0_fun/ppermute | solution.py:53
